TPU v7x, 32 devices: a whole 2x2x4 slice. The times are simulated.
32 devices in a mesh: gx: 4 (over z), yz: 8 (over y, x, core).
Axes of the slice: x: 2, y: 2, z: 4, core: 2. Of those that a mesh axis runs over, the one named last changes fastest.
Arguments:
- features: bfloat16 [384, 96, 512], P(('gx', 'yz')), may hold values from -6 to 6
- occupancy: int32 [384, 512], P(('gx', 'yz')), may hold values 0 or 1
- neighbours: int32 [384, 27], P(('gx', 'yz')), may hold values from 0 to 84, as said below
- exports: int32 [256], P(('gx', 'yz')), may hold values from 0 to 11, as said below
- coarse_map: int32 [384, 2], P(('gx', 'yz')), may hold values from 0 to 7, as said below
- owners: int32 [128], P(('gx', 'yz')), may hold values from 0 to 7, as said below
- w_sub: bfloat16 [27, 96, 96], replicated, may hold values from -0.15625 to 0.15625
- w_down: bfloat16 [8, 192, 96], replicated, may hold values from -0.3125 to 0.3125
- cotangent: bfloat16 [256, 192, 512], P(('gx', 'yz')), may hold values from -6 to 6
Outputs:
- coarse: bfloat16 [256, 192, 512], P(('gx', 'yz'))
- grad_features: bfloat16 [384, 96, 512], P(('gx', 'yz'))
- grad_sub: float32 [27, 96, 96], replicated
- grad_down: float32 [8, 192, 96], replicated
Inputs may be any that keep to these rules, and one draw needn't show every extreme that they name: `neighbours`: entry 13 of a brick is its own slot. Entries follow the geometry of a map of 8-voxel bricks in which device (i, j) holds a region of 4 x 4 x 2 brick cells beside the regions of (i +- 1, j +- 1); a brick met at offset k meets the first at the opposite offset. Entries that point to another device name only bricks on that device's side faces. `exports`: each device's 8 entries are distinct slots of its bricks that lie on its region's side faces, and every such brick is listed. `coarse_map`: column 0 is the coarse cell (0 to 3), column 1 the octant; every coarse cell of every device holds exactly 3 of its fine bricks, in distinct octants. The 4 coarse cells of one device have distinct owners; in every gx slab one owner is named by every device of the slab.
All inputs are finite; a program needn't handle non-finite values. No bound on the sum of `occupancy` on one device may be relied on, other than what follows from the above.
Results may differ from a plain program's by a relative error of at most 0.0062.
Values may be sent and summed in bfloat16 or wider, within the bound.
A program may use at most 320 MiB of HBM per device.

v0:
```python
import jax
import jax.numpy as jnp
from jax import lax
from jax.sharding import PartitionSpec as P

EDGE = 8


def padded_2(x, sides, width):
    for axis, dim in sides:
        size, length = (lax.axis_size(axis), x.shape[dim])
        up = [(i, (i + 1) % size) for i in range(size - 1)]
        down = [(j, i) for i, j in up]
        last = lax.slice_in_dim(x, length - width, length, axis=dim)
        initial = lax.slice_in_dim(x, 0, width, axis=dim)
        before = lax.ppermute(last, axis, up)
        after = lax.ppermute(initial, axis, down)
        x = jnp.concatenate([before, x, after], axis=dim)
    return x


def silu_slope(values):
    sig = jax.nn.sigmoid(values)
    return sig * (1.0 + values * (1.0 - sig))


def layer_span(shift, cube_edge):
    if shift < 0:
        return (slice(cube_edge - 1, cube_edge), slice(0, 1))
    if shift > 0:
        return (slice(0, 1), slice(cube_edge + 1, cube_edge + 2))
    return (slice(0, cube_edge), slice(1, cube_edge + 1))


def pad_bricks(lookup, neighbour_ids, cube_edge):
    channels = lookup.shape[1]
    blocks = lookup.reshape(lookup.shape[0], channels, cube_edge, cube_edge, cube_edge)
    padded = jnp.zeros(
        (neighbour_ids.shape[0], channels, cube_edge + 2, cube_edge + 2, cube_edge + 2),
        lookup.dtype,
    )
    for offset in range(27):
        spans = [
            layer_span(shift, cube_edge)
            for shift in (offset // 9 - 1, offset // 3 % 3 - 1, offset % 3 - 1)
        ]
        facing = blocks[:, :, spans[0][0], spans[1][0], spans[2][0]]
        picked = jnp.take(facing, neighbour_ids[:, offset], axis=0)
        padded = padded.at[:, :, spans[0][1], spans[1][1], spans[2][1]].set(picked)
    return padded


def conv_forward(padded, weights, cube_edge):
    result = None
    for offset in range(27):
        start_x, start_y, start_z = (offset // 9, offset // 3 % 3, offset % 3)
        window = padded[
            :,
            :,
            start_x : start_x + cube_edge,
            start_y : start_y + cube_edge,
            start_z : start_z + cube_edge,
        ]
        term = jnp.einsum(
            "oi,bixyz->boxyz", weights[offset], window, preferred_element_type=jnp.float32
        )
        result = term if result is None else result + term
    return result


def conv_transpose(padded, weights, cube_edge):
    result = None
    for offset in range(27):
        start_x, start_y, start_z = (2 - offset // 9, 2 - offset // 3 % 3, 2 - offset % 3)
        window = padded[
            :,
            :,
            start_x : start_x + cube_edge,
            start_y : start_y + cube_edge,
            start_z : start_z + cube_edge,
        ]
        term = jnp.einsum(
            "oi,boxyz->bixyz", weights[offset], window, preferred_element_type=jnp.float32
        )
        result = term if result is None else result + term
    return result


def conv_weights(padded, grads, cube_edge):
    terms = []
    for offset in range(27):
        start_x, start_y, start_z = (offset // 9, offset // 3 % 3, offset % 3)
        window = padded[
            :,
            :,
            start_x : start_x + cube_edge,
            start_y : start_y + cube_edge,
            start_z : start_z + cube_edge,
        ]
        terms.append(
            jnp.einsum("boxyz,bixyz->oi", grads, window, preferred_element_type=jnp.float32)
        )
    return jnp.stack(terms)


def split_fine(values, half_edge):
    rows, channels = (values.shape[0], values.shape[1])
    shaped = values.reshape(rows, channels, half_edge, 2, half_edge, 2, half_edge, 2)
    return shaped.transpose(0, 1, 3, 5, 7, 2, 4, 6).reshape(rows, channels, 8, half_edge**3)


def join_fine(values, half_edge):
    rows, channels = (values.shape[0], values.shape[1])
    shaped = values.reshape(rows, channels, 2, 2, 2, half_edge, half_edge, half_edge)
    return shaped.transpose(0, 1, 5, 2, 6, 3, 7, 4).reshape(rows, channels, 8 * half_edge**3)


def split_block(values, half_edge):
    rows, channels = (values.shape[0], values.shape[1])
    shaped = values.reshape(rows, channels, 2, half_edge, 2, half_edge, 2, half_edge)
    return shaped.transpose(0, 1, 2, 4, 6, 3, 5, 7).reshape(rows, channels, 8, half_edge**3)


def join_block(values, half_edge):
    rows, channels = (values.shape[0], values.shape[1])
    shaped = values.reshape(rows, channels, 2, 2, 2, half_edge, half_edge, half_edge)
    return shaped.transpose(0, 1, 2, 5, 3, 6, 4, 7).reshape(rows, channels, 8 * half_edge**3)


def rim_lookup(own_bricks, exports, forward):
    voxels = own_bricks.shape[2]
    outgoing = jnp.take(own_bricks, exports, axis=0)
    if forward:
        arrived = padded_2(outgoing[None, None], (("gx", 0), ("yz", 1)), 1)
    else:
        arrived = padded_2(outgoing[None, None], (("gx", 0), ("yz", 1)), 1)
    arrived = arrived.reshape(-1, own_bricks.shape[1], voxels)
    blank = jnp.zeros((1, own_bricks.shape[1], voxels), own_bricks.dtype)
    return jnp.concatenate([own_bricks, arrived, blank], axis=0)


def activate_coarse(coarse_pre, cotangent):
    coarse_wide = coarse_pre.astype(jnp.float32)
    grad_coarse = (cotangent.astype(jnp.float32) * silu_slope(coarse_wide)).astype(jnp.bfloat16)
    return grad_coarse


def on_device(
    features, occupancy, neighbours, exports, coarse_map, owners, w_sub, w_down, cotangent
):
    bricks = features.shape[0]
    channels = features.shape[1]
    voxels = features.shape[2]
    half_edge = EDGE // 2
    groups = lax.axis_size("yz")
    live = occupancy.astype(jnp.float32).reshape(bricks, 1, EDGE, EDGE, EDGE)
    masked = features * occupancy.astype(jnp.bfloat16)[:, None, :]
    padded_input = pad_bricks(rim_lookup(masked, exports, True), neighbours, EDGE)
    pre_sub = conv_forward(padded_input, w_sub, EDGE) * live
    hidden = jax.nn.silu(pre_sub).astype(jnp.bfloat16)
    strided = split_fine(hidden.reshape(bricks, channels, voxels), half_edge)
    piece = jnp.einsum("toi,bitu->bou", w_down, strided, preferred_element_type=jnp.float32).astype(
        jnp.bfloat16
    )
    cell_of = coarse_map[:, 0]
    octant_of = coarse_map[:, 1]
    owner_of = jnp.take(owners, cell_of)
    group_ids = jnp.arange(groups, dtype=jnp.int32)
    octant_ids = jnp.arange(8, dtype=jnp.int32)
    select = (
        (owner_of[None, None, :] == group_ids[:, None, None])
        & (octant_of[None, None, :] == octant_ids[None, :, None])
    ).astype(jnp.bfloat16)
    outgoing = join_block(
        jnp.einsum("gob,bcu->gcou", select, piece, preferred_element_type=jnp.float32).astype(
            jnp.bfloat16
        ),
        half_edge,
    )
    coarse_pre = lax.all_to_all(outgoing, "yz", split_axis=0, concat_axis=0, tiled=True)
    grad_coarse = activate_coarse(coarse_pre, cotangent)
    returned = split_block(
        lax.all_to_all(grad_coarse, "yz", split_axis=0, concat_axis=0, tiled=True), half_edge
    )
    grad_piece = jnp.einsum(
        "gob,gcou->bcu", select, returned, preferred_element_type=jnp.float32
    ).astype(jnp.bfloat16)
    coarse = jax.nn.silu(coarse_pre.astype(jnp.float32)).astype(jnp.bfloat16)
    down_local = jnp.einsum(
        "bou,bitu->toi", grad_piece, strided, preferred_element_type=jnp.float32
    )
    grad_hidden = join_fine(
        jnp.einsum("toi,bou->bitu", w_down, grad_piece, preferred_element_type=jnp.float32),
        half_edge,
    )
    grad_hidden = grad_hidden.reshape(bricks, channels, EDGE, EDGE, EDGE)
    grad_pre = (grad_hidden * silu_slope(pre_sub) * live).astype(jnp.bfloat16)
    padded_grad = pad_bricks(
        rim_lookup(grad_pre.reshape(bricks, channels, voxels), exports, False), neighbours, EDGE
    )
    grad_input = conv_transpose(padded_grad, w_sub, EDGE) * live
    grad_features = grad_input.reshape(bricks, channels, voxels).astype(jnp.bfloat16)
    sub_local = conv_weights(padded_input, grad_pre, EDGE)
    grad_sub, grad_down = lax.psum((sub_local, down_local), ("gx", "yz"))
    return (coarse, grad_features, grad_sub, grad_down)


def solution(mesh):
    in_specs = (
        P(("gx", "yz"), None, None),
        P(("gx", "yz"), None),
        P(("gx", "yz"), None),
        P(("gx", "yz")),
        P(("gx", "yz"), None),
        P(("gx", "yz")),
        P(),
        P(),
        P(("gx", "yz"), None, None),
    )
    out_specs = (P(("gx", "yz"), None, None), P(("gx", "yz"), None, None), P(), P())
    return jax.shard_map(
        on_device, mesh=mesh, in_specs=in_specs, out_specs=out_specs, check_vma=False
    )
```

profile of v0, /device:TPU:0, one launch (start us, length us, event | category | flops | bytes accessed | tf_op | source)
XLA Modules:
  0.0 806.1 jit_solution(12787594770374967149)
XLA Ops:
  13.5 6.5 collective-permute-start
  38.3 3.1 pad_maximum_fusion.2
  42.7 4.5 collective-permute-start.2
  47.9 3.3 copy.305
  66.5 6.2 pad_maximum_fusion
  72.7 12.1 %copy.306 = bf16[3,3,8,96,512]{3,2,1,0,4:T(8,128)(2,1)} copy(bf16[3,3,8,96,512]{4,3,2,1,0:T(8,128)(2,1)} %pad_maximum_fusion) | data formatting | bytes 14155776 | tf_op jit(solution)/shard_map/concatenate | solution.py:18
  84.8 8.6 %maximum_maximum_fusion = bf16[85,96,8,8,8]{1,0,4,3,2:T(8,128)(2,1)S(1)} fusion(bf16[72,96,8,8,8]{1,0,4,3,2:T(8,128)(2,1)} %bitcast.1018, bf16[12,96,8,8,8]{1,0,4,3,2:T(8,128)(2,1)S(1)} %bitcast.1024, bf16[85]{0:T(256)(128)(2,1)S(1)} %copy-done.96), kind=kLoop, calls=%fused_computation.57 | loop fusion | flops 25067520 | bytes 16613546 | tf_op jit(solution)/shard_map/concatenate | solution.py:139
  95.0 6.4 copy.325
  144.0 5.1 gather_fusion.15
  170.6 4.2 fusion.66
  184.3 4.5 fusion.281
  194.2 2.8 fusion.293
  205.1 2.8 fusion.309
  207.9 3.1 fusion.313
  211.0 2.8 fusion.317
  216.5 2.8 fusion.325
  227.3 2.8 fusion.341
  238.2 2.8 fusion.357
  249.2 2.8 fusion.373
  257.4 37.2 %multiply_convert_fusion.1 = (bf16[12,96,8,8,8]{1,0,4,3,2:T(8,128)(2,1)S(1)}, f32[12,96,8,8,8]{1,0,4,3,2:T(8,128)}) fusion(f32[12,8,8,8]{0,3,2,1:T(8,128)S(1)} %bitcast.1029, bf16[12,96,10,10,10]{1,0,4,3,2:T(8,128)(2,1)} %constant_dynamic-update-slice_fusion.7, bf16[27,96,96]{2,1,0:T(8,128)(2,1)} %param.141, f32[12,8,8,8,96]{4,0,3,2,1:T(8,128)} %fusion.281, ...), kind=kOutput, calls=%fused_computation.88 | convolution fusion | flops 132120576 | bytes 116736000 | tf_op jit(solution)/shard_map/oi,bixyz->boxyz/dot_general | solution.py:64
  302.5 2.8 copy.349
  305.3 55.4 %all_to_all.10 = bf16[8,192,512]{2,1,0:T(8,128)(2,1)S(1)} all-to-all(bf16[8,192,512]{2,1,0:T(8,128)(2,1)} %copy.349), channel_id=1, replica_groups=mesh['gx'=4,'yz'=8] {'yz'}, dimensions={0} | all-to-all | bytes 3145728 | tf_op jit(solution)/shard_map/all_to_all | solution.py:180
  360.7 3.2 fusion.10
  363.9 4.3 all-to-all-start.1
  368.2 4.2 copy.395
  372.4 16.8 %all-to-all-done.1 = bf16[8,192,512]{2,1,0:T(8,128)(2,1)} async-done(((bf16[8,192,512]{2,1,0:T(8,128)(2,1)}), bf16[8,192,512]{2,1,0:T(8,128)(2,1)}, u32[]{:S(2)}, u32[]{:S(2)}) %all-to-all-start.1) | async-done | bytes 1572896 | tf_op jit(solution)/shard_map/all_to_all | solution.py:183
  389.2 3.2 copy.350
  392.4 3.5 copy.351
  396.0 3.6 reshape.2536
  407.3 2.9 gather_fusion.29
  413.1 5.0 collective-permute-start.4
  418.1 3.0 fusion.72
  456.2 4.5 collective-permute-start.6
  466.5 132.7 %all-reduce.5.cloned.1.call-done = (f32[27,96,96]{2,1,0:T(8,128)}, f32[8,192,96]{1,0,2:T(8,128)}) async-done(((f32[27,96,96]{2,1,0:T(8,128)}, f32[8,192,96]{1,0,2:T(8,128)}), (f32[27,96,96]{2,1,0:T(8,128)}, f32[8,192,96]{1,0,2:T(8,128)})) %all-reduce.5.cloned.1.call-update) | async-done | bytes 1585168 | tf_op jit(solution)/shard_map/psum | solution.py:204
  601.5 6.2 pad_maximum_fusion.1
  607.8 12.1 %copy.460 = bf16[3,3,8,96,512]{3,2,1,0,4:T(8,128)(2,1)} copy(bf16[3,3,8,96,512]{4,3,2,1,0:T(8,128)(2,1)} %pad_maximum_fusion.1) | data formatting | bytes 14155776 | tf_op jit(solution)/shard_map/concatenate | solution.py:139
  619.8 8.6 %maximum_maximum_fusion.1 = bf16[85,96,8,8,8]{1,0,4,3,2:T(8,128)(2,1)S(1)} fusion(bf16[72,96,8,8,8]{1,0,4,3,2:T(8,128)(2,1)} %bitcast.1017, bf16[12,96,8,8,8]{1,0,4,3,2:T(8,128)(2,1)S(1)} %multiply_convert_fusion, bf16[85]{0:T(256)(128)(2,1)S(1)} %copy-done.97), kind=kLoop, calls=%fused_computation.58 | loop fusion | flops 25067520 | bytes 16613546 | tf_op jit(solution)/shard_map/concatenate | solution.py:139
  634.5 6.3 copy.375
  666.3 5.1 gather_fusion.43
  671.5 2.8 copy.381
  676.4 2.8 copy.369
  687.4 3.1 fusion.279
  693.2 2.8 fusion.287
  704.0 2.8 fusion.303
  709.4 3.0 fusion.311
  736.8 2.8 fusion.351
  747.7 2.8 fusion.367
  758.6 35.2 %fusion.1 = bf16[12,96,8,8,8]{1,0,4,3,2:T(8,128)(2,1)S(1)} fusion(f32[12,8,8,8,96]{4,0,3,2,1:T(8,128)} %fusion.279, f32[12,8,8,8,96]{4,0,3,2,1:T(8,128)} %fusion.283, f32[12,8,8,8,96]{4,0,3,2,1:T(8,128)} %fusion.287, f32[12,8,8,8,96]{4,0,3,2,1:T(8,128)} %fusion.291, f32[12,8,8,8,96]{4,0,3,2,1:T(8,128)} %fusion.295, f32[12,8,8,8,96]{4,0,3,2,1:T(8,128)} %fusion.299, ...), kind=kOutput, calls=%fused_computation.66 | convolution fusion | flops 129761280 | bytes 114376704 | tf_op jit(solution)/shard_map/oi,boxyz->bixyz/dot_general | solution.py:82
  (523 shorter events, 324.1 us)
Async XLA Ops:
  7.2 289.4 %copy-start = (bf16[8,192,96]{2,1,0:T(8,128)(2,1)S(1)}, bf16[8,192,96]{2,1,0:T(8,128)(2,1)}, u32[]{:S(2)}) copy-start(bf16[8,192,96]{2,1,0:T(8,128)(2,1)} %param.142) | copy-start | bytes 884740
  7.9 33.5 %copy-start.98 = (pred[8]{0:T(512)(128)(4,1)}, pred[8]{0:T(512)(128)(4,1)S(1)}, u32[]{:S(2)}) copy-start(pred[8]{0:T(512)(128)(4,1)S(1)} %compare_and_fusion.27) | copy-start | bytes 28
  8.6 32.8 %copy-start.33 = (s32[1024]{0:T(1024)}, s32[1024]{0:T(1024)S(1)}, u32[]{:S(2)}) copy-start(s32[1024]{0:T(1024)S(1)} %pad_clamp_fusion.28) | copy-start | bytes 12292
  11.4 30.0 %copy-start.8 = (bf16[12,96,512]{2,1,0:T(8,128)(2,1)}, bf16[12,96,512]{2,1,0:T(8,128)(2,1)S(1)}, u32[]{:S(2)}) copy-start(bf16[12,96,512]{2,1,0:T(8,128)(2,1)S(1)} %broadcast_multiply_fusion) | copy-start | bytes 3538948
  12.2 26.1 %collective-permute-start.1 = (bf16[1,1,8,96,512]{4,3,2,1,0:T(8,128)(2,1)S(1)}, bf16[1,1,8,96,512]{4,3,2,1,0:T(8,128)(2,1)S(1)}, u32[]{:S(2)}, u32[]{:S(2)}) collective-permute-start(bf16[1,1,8,96,512]{4,3,2,1,0:T(8,128)(2,1)S(1)} %select_bitcast_fusion.1), channel_id=1, source_target_pairs={{8,0},{16,8},{24,16},{9,1},{17,9},{25,17},{10,2},{18,10},{26,18},{... | collective-permute-start | bytes 2359304 | tf_op jit(solution)/shard_map/ppermute | solution.py:17
  13.5 24.8 %collective-permute-start = (bf16[1,1,8,96,512]{4,3,2,1,0:T(8,128)(2,1)S(1)}, bf16[1,1,8,96,512]{4,3,2,1,0:T(8,128)(2,1)}, u32[]{:S(2)}, u32[]{:S(2)}) collective-permute-start(bf16[1,1,8,96,512]{4,3,2,1,0:T(8,128)(2,1)S(1)} %select_bitcast_fusion.1), channel_id=1, source_target_pairs={{0,8},{8,16},{16,24},{1,9},{9,17},{17,25},{2,10},{10,18},{18,26},{... | collective-permute-start | bytes 2359304 | tf_op jit(solution)/shard_map/ppermute | solution.py:16
  20.3 26.9 %copy-start.52 = (s32[12]{0:T(128)}, s32[12]{0:T(128)S(1)}, u32[]{:S(2)}) copy-start(s32[12]{0:T(128)S(1)} %get-tuple-element.700) | copy-start | bytes 148
  20.3 26.9 %copy-start.70 = (s32[12]{0:T(128)}, s32[12]{0:T(128)S(1)}, u32[]{:S(2)}) copy-start(s32[12]{0:T(128)S(1)} %get-tuple-element.699) | copy-start | bytes 148
  20.8 26.3 %copy-start.53 = (s32[12]{0:T(128)}, s32[12]{0:T(128)S(1)}, u32[]{:S(2)}) copy-start(s32[12]{0:T(128)S(1)} %get-tuple-element.698) | copy-start | bytes 148
  20.9 26.3 %copy-start.54 = (s32[12]{0:T(128)}, s32[12]{0:T(128)S(1)}, u32[]{:S(2)}) copy-start(s32[12]{0:T(128)S(1)} %get-tuple-element.696) | copy-start | bytes 148
  20.9 26.3 %copy-start.55 = (s32[12]{0:T(128)}, s32[12]{0:T(128)S(1)}, u32[]{:S(2)}) copy-start(s32[12]{0:T(128)S(1)} %get-tuple-element.697) | copy-start | bytes 148
  20.9 26.3 %copy-start.56 = (s32[12]{0:T(128)}, s32[12]{0:T(128)S(1)}, u32[]{:S(2)}) copy-start(s32[12]{0:T(128)S(1)} %get-tuple-element.694) | copy-start | bytes 148
  20.9 26.3 %copy-start.57 = (s32[12]{0:T(128)}, s32[12]{0:T(128)S(1)}, u32[]{:S(2)}) copy-start(s32[12]{0:T(128)S(1)} %get-tuple-element.695) | copy-start | bytes 148
  20.9 26.3 %copy-start.58 = (s32[12]{0:T(128)}, s32[12]{0:T(128)S(1)}, u32[]{:S(2)}) copy-start(s32[12]{0:T(128)S(1)} %get-tuple-element.692) | copy-start | bytes 148
  20.9 26.3 %copy-start.59 = (s32[12]{0:T(128)}, s32[12]{0:T(128)S(1)}, u32[]{:S(2)}) copy-start(s32[12]{0:T(128)S(1)} %get-tuple-element.693) | copy-start | bytes 148
  20.9 26.3 %copy-start.60 = (s32[12]{0:T(128)}, s32[12]{0:T(128)S(1)}, u32[]{:S(2)}) copy-start(s32[12]{0:T(128)S(1)} %get-tuple-element.690) | copy-start | bytes 148
  20.9 26.3 %copy-start.61 = (s32[12]{0:T(128)}, s32[12]{0:T(128)S(1)}, u32[]{:S(2)}) copy-start(s32[12]{0:T(128)S(1)} %get-tuple-element.691) | copy-start | bytes 148
  20.9 26.3 %copy-start.62 = (s32[12]{0:T(128)}, s32[12]{0:T(128)S(1)}, u32[]{:S(2)}) copy-start(s32[12]{0:T(128)S(1)} %get-tuple-element.688) | copy-start | bytes 148
  20.9 26.3 %copy-start.63 = (s32[12]{0:T(128)}, s32[12]{0:T(128)S(1)}, u32[]{:S(2)}) copy-start(s32[12]{0:T(128)S(1)} %get-tuple-element.689) | copy-start | bytes 148
  21.0 26.3 %copy-start.66 = (s32[12]{0:T(128)}, s32[12]{0:T(128)S(1)}, u32[]{:S(2)}) copy-start(s32[12]{0:T(128)S(1)} %get-tuple-element.684) | copy-start | bytes 148
  21.0 26.3 %copy-start.67 = (s32[12]{0:T(128)}, s32[12]{0:T(128)S(1)}, u32[]{:S(2)}) copy-start(s32[12]{0:T(128)S(1)} %get-tuple-element.685) | copy-start | bytes 148
  21.0 26.3 %copy-start.68 = (s32[12]{0:T(128)}, s32[12]{0:T(128)S(1)}, u32[]{:S(2)}) copy-start(s32[12]{0:T(128)S(1)} %get-tuple-element.682) | copy-start | bytes 148
  21.0 26.3 %copy-start.69 = (s32[12]{0:T(128)}, s32[12]{0:T(128)S(1)}, u32[]{:S(2)}) copy-start(s32[12]{0:T(128)S(1)} %get-tuple-element.683) | copy-start | bytes 148
  21.0 26.3 %copy-start.71 = (s32[12]{0:T(128)}, s32[12]{0:T(128)S(1)}, u32[]{:S(2)}) copy-start(s32[12]{0:T(128)S(1)} %get-tuple-element.681) | copy-start | bytes 148
  25.2 87.7 %copy-start.29 = (s32[1024]{0:T(1024)}, s32[1024]{0:T(1024)S(1)}, u32[]{:S(2)}) copy-start(s32[1024]{0:T(1024)S(1)} %pad_clamp_fusion.27) | copy-start | bytes 12292
  30.0 88.1 %copy-start.30 = (s32[1024]{0:T(1024)}, s32[1024]{0:T(1024)S(1)}, u32[]{:S(2)}) copy-start(s32[1024]{0:T(1024)S(1)} %pad_clamp_fusion.9) | copy-start | bytes 12292
  30.0 87.5 %copy-start.31 = (s32[1024]{0:T(1024)}, s32[1024]{0:T(1024)S(1)}, u32[]{:S(2)}) copy-start(s32[1024]{0:T(1024)S(1)} %pad_clamp_fusion.7) | copy-start | bytes 12292
  30.7 86.2 %copy-start.32 = (s32[1024]{0:T(1024)}, s32[1024]{0:T(1024)S(1)}, u32[]{:S(2)}) copy-start(s32[1024]{0:T(1024)S(1)} %pad_clamp_fusion.3) | copy-start | bytes 12292
  41.4 25.0 %collective-permute-start.3 = (bf16[3,1,8,96,512]{4,3,2,1,0:T(8,128)(2,1)}, bf16[3,1,8,96,512]{4,3,2,1,0:T(8,128)(2,1)}, u32[]{:S(2)}, u32[]{:S(2)}) collective-permute-start(bf16[3,1,8,96,512]{4,3,2,1,0:T(8,128)(2,1)} %pad_maximum_fusion.2), channel_id=1, source_target_pairs={{1,0},{2,1},{3,2},{4,3},{5,4},{6,5},{7,6},{9,8},{10,9},{11,10},{12... | collective-permute-start | bytes 7077896 | tf_op jit(solution)/shard_map/ppermute | solution.py:17
  42.7 23.7 %collective-permute-start.2 = (bf16[3,1,8,96,512]{4,3,2,1,0:T(8,128)(2,1)}, bf16[3,1,8,96,512]{4,3,2,1,0:T(8,128)(2,1)}, u32[]{:S(2)}, u32[]{:S(2)}) collective-permute-start(bf16[3,1,8,96,512]{4,3,2,1,0:T(8,128)(2,1)} %pad_maximum_fusion.2), channel_id=1, source_target_pairs={{0,1},{1,2},{2,3},{3,4},{4,5},{5,6},{6,7},{8,9},{9,10},{10,11},{11... | collective-permute-start | bytes 7077896 | tf_op jit(solution)/shard_map/ppermute | solution.py:16
  52.1 350.5 %copy-start.12 = (f32[12,512]{0,1:T(8,128)}, f32[12,512]{0,1:T(8,128)S(1)}, u32[]{:S(2)}) copy-start(f32[12,512]{0,1:T(8,128)S(1)} %copy.457) | copy-start | bytes 73732
  153.4 25.9 %copy-start.77 = (pred[12]{0:T(512)(128)(4,1)S(1)}, pred[12]{0:T(512)(128)(4,1)}, u32[]{:S(2)}) copy-start(pred[12]{0:T(512)(128)(4,1)} %get-tuple-element.804) | copy-start | bytes 40
  153.4 26.5 %copy-start.38 = (pred[12]{0:T(512)(128)(4,1)S(1)}, pred[12]{0:T(512)(128)(4,1)}, u32[]{:S(2)}) copy-start(pred[12]{0:T(512)(128)(4,1)} %get-tuple-element.803) | copy-start | bytes 40
  153.4 27.3 %copy-start.83 = (pred[12]{0:T(512)(128)(4,1)S(1)}, pred[12]{0:T(512)(128)(4,1)}, u32[]{:S(2)}) copy-start(pred[12]{0:T(512)(128)(4,1)} %get-tuple-element.802) | copy-start | bytes 40
  153.4 28.1 %copy-start.36 = (pred[12]{0:T(512)(128)(4,1)S(1)}, pred[12]{0:T(512)(128)(4,1)}, u32[]{:S(2)}) copy-start(pred[12]{0:T(512)(128)(4,1)} %get-tuple-element.801) | copy-start | bytes 40
  153.4 28.8 %copy-start.74 = (pred[12]{0:T(512)(128)(4,1)S(1)}, pred[12]{0:T(512)(128)(4,1)}, u32[]{:S(2)}) copy-start(pred[12]{0:T(512)(128)(4,1)} %get-tuple-element.800) | copy-start | bytes 40
  153.4 29.5 %copy-start.34 = (pred[12]{0:T(512)(128)(4,1)S(1)}, pred[12]{0:T(512)(128)(4,1)}, u32[]{:S(2)}) copy-start(pred[12]{0:T(512)(128)(4,1)} %get-tuple-element.799) | copy-start | bytes 40
  153.4 30.2 %copy-start.72 = (pred[12]{0:T(512)(128)(4,1)S(1)}, pred[12]{0:T(512)(128)(4,1)}, u32[]{:S(2)}) copy-start(pred[12]{0:T(512)(128)(4,1)} %get-tuple-element.798) | copy-start | bytes 40
  153.4 30.8 %copy-start.18 = (bf16[27,96,96]{2,1,0:T(8,128)(2,1)S(1)}, bf16[27,96,96]{2,1,0:T(8,128)(2,1)}, u32[]{:S(2)}) copy-start(bf16[27,96,96]{2,1,0:T(8,128)(2,1)} %param.141) | copy-start | bytes 1492996
  305.3 55.4 %copy-start.23 = (bf16[8,192,512]{2,1,0:T(8,128)(2,1)S(1)}, bf16[8,192,512]{2,1,0:T(8,128)(2,1)}, u32[]{:S(2)}) copy-start(bf16[8,192,512]{2,1,0:T(8,128)(2,1)} %param.143) | copy-start | bytes 4718596
  363.9 25.4 %all-to-all-start.1 = ((bf16[8,192,512]{2,1,0:T(8,128)(2,1)}), bf16[8,192,512]{2,1,0:T(8,128)(2,1)}, u32[]{:S(2)}, u32[]{:S(2)}) async-start(bf16[8,192,512]{2,1,0:T(8,128)(2,1)} %get-tuple-element.762), calls=%async_computation.1 | async-start | bytes 3145728 | tf_op jit(solution)/shard_map/all_to_all | solution.py:183
  368.2 231.0 %all-reduce.5.cloned.1.call-start = ((), (), s32[]{:S(2)}) async-start(), calls=%async_computation.2 | async-start | bytes 4227072 | tf_op jit(solution)/shard_map/psum | solution.py:204
  411.5 41.6 %collective-permute-start.5 = (bf16[1,1,8,96,512]{4,3,2,1,0:T(8,128)(2,1)S(1)}, bf16[1,1,8,96,512]{4,3,2,1,0:T(8,128)(2,1)S(1)}, u32[]{:S(2)}, u32[]{:S(2)}) collective-permute-start(bf16[1,1,8,96,512]{4,3,2,1,0:T(8,128)(2,1)S(1)} %select_bitcast_fusion), channel_id=1, source_target_pairs={{8,0},{16,8},{24,16},{9,1},{17,9},{25,17},{10,2},{18,10},{26,18},{... | collective-permute-start | bytes 2359304 | tf_op jit(solution)/shard_map/ppermute | solution.py:17
  413.1 40.0 %collective-permute-start.4 = (bf16[1,1,8,96,512]{4,3,2,1,0:T(8,128)(2,1)S(1)}, bf16[1,1,8,96,512]{4,3,2,1,0:T(8,128)(2,1)S(1)}, u32[]{:S(2)}, u32[]{:S(2)}) collective-permute-start(bf16[1,1,8,96,512]{4,3,2,1,0:T(8,128)(2,1)S(1)} %select_bitcast_fusion), channel_id=1, source_target_pairs={{0,8},{8,16},{16,24},{1,9},{9,17},{17,25},{2,10},{10,18},{18,26},{... | collective-permute-start | bytes 2359304 | tf_op jit(solution)/shard_map/ppermute | solution.py:16
  454.8 146.7 %collective-permute-start.7 = (bf16[3,1,8,96,512]{4,3,2,1,0:T(8,128)(2,1)}, bf16[3,1,8,96,512]{4,3,2,1,0:T(8,128)(2,1)}, u32[]{:S(2)}, u32[]{:S(2)}) collective-permute-start(bf16[3,1,8,96,512]{4,3,2,1,0:T(8,128)(2,1)} %pad_maximum_fusion.3), channel_id=1, source_target_pairs={{1,0},{2,1},{3,2},{4,3},{5,4},{6,5},{7,6},{9,8},{10,9},{11,10},{12... | collective-permute-start | bytes 7077896 | tf_op jit(solution)/shard_map/ppermute | solution.py:17
  456.2 145.3 %collective-permute-start.6 = (bf16[3,1,8,96,512]{4,3,2,1,0:T(8,128)(2,1)}, bf16[3,1,8,96,512]{4,3,2,1,0:T(8,128)(2,1)}, u32[]{:S(2)}, u32[]{:S(2)}) collective-permute-start(bf16[3,1,8,96,512]{4,3,2,1,0:T(8,128)(2,1)} %pad_maximum_fusion.3), channel_id=1, source_target_pairs={{0,1},{1,2},{2,3},{3,4},{4,5},{5,6},{6,7},{8,9},{9,10},{10,11},{11... | collective-permute-start | bytes 7077896 | tf_op jit(solution)/shard_map/ppermute | solution.py:16
  687.4 68.5 %copy-start.4 = (bf16[12,96,10,10,10]{1,0,4,3,2:T(8,128)(2,1)}, bf16[12,96,10,10,10]{1,0,4,3,2:T(8,128)(2,1)S(1)}, u32[]{:S(2)}) copy-start(bf16[12,96,10,10,10]{1,0,4,3,2:T(8,128)(2,1)S(1)} %constant_dynamic-update-slice_fusion) | copy-start | bytes 6912004
  758.6 40.2 %copy-start.1 = (bf16[8,192,96]{2,1,0:T(8,128)(2,1)S(1)}, bf16[8,192,96]{2,1,0:T(8,128)(2,1)}, u32[]{:S(2)}) copy-start(bf16[8,192,96]{2,1,0:T(8,128)(2,1)} %param.142) | copy-start | bytes 884740
  (64 other events, 484.8 us)
Sparse Core Ops, SparseCore 0:
  466.7 132.4 all-reduce.4
where the time goes:
time: 815 us; the launch traced here: 806 us
  matrix products  260 us (32%)
  local copies, waits for them, and re-layouts  183 us (22%)
  waiting for transfers between devices  149 us (18%)
  other arithmetic  112 us (14%)
  blocking collectives  55.4 us (7%)
  starting transfers between devices  30.3 us (4%)
  between operations  16.4 us (2%)
    psum x1, waiting for transfers between devices, on_device(): grad_sub, grad_down = lax.psum((sub_local, down_local), ('gx', 'yz'))  133 us
    dot_general x27, matrix products, conv_forward(): jnp.einsum('oi,bixyz->boxyz', weights[offset], window, preferred_element_...  110 us
    dot_general x27, matrix products, conv_transpose(): jnp.einsum('oi,boxyz->bixyz', weights[offset], window, preferred_element_...  106 us
    gather x54, local copies, waits for them, and re-layouts, pad_bricks(): picked = jnp.take(facing, neighbour_ids[:, offset], axis=0)  63.4 us
    all_to_all x1, blocking collectives, on_device(): lax.all_to_all(outgoing, 'yz', split_axis=0, concat_axis=0, tiled=True)  55.4 us
    dot_general x27, matrix products, conv_weights(): jnp.einsum('boxyz,bixyz->oi', grads, window, preferred_element_type=jnp.f...  39.1 us
    scatter x52, other arithmetic, pad_bricks(): padded = padded.at[:, :, spans[0][1], spans[1][1], spans[2][1]].set(picked)  35.7 us
    another operation x50, local copies, waits for them, and re-layouts, pad_bricks(): picked = jnp.take(facing, neighbour_ids[:, offset], axis=0)  33.3 us
  transfers between devices with their start and end apart: 10, of which 2 were waited for; matrix products, arithmetic and copies ran while one was open for 10% of the time, Pallas kernels for 0%

commit v1 on v0

v1 whole, which is shorter than its diff:
```python
import jax
import jax.numpy as jnp
import numpy as np
from jax import lax
from jax.experimental import pallas as pl
from jax.experimental.pallas import tpu as pltpu
from jax.sharding import PartitionSpec as P

EDGE = 8
VOX = 512
LANES = 128
TAPS = 27
VMEM_BYTES = 56 * 2**20


def silu_slope(values):
    sig = jax.nn.sigmoid(values)
    return sig * (1.0 + values * (1.0 - sig))


def fine_order():
    ids = np.arange(VOX).reshape(4, 2, 4, 2, 4, 2).transpose(1, 3, 5, 0, 2, 4).reshape(-1)
    return np.eye(VOX, dtype=np.float32)[ids]


def block_order():
    ids = np.arange(VOX).reshape(2, 4, 2, 4, 2, 4).transpose(0, 2, 4, 1, 3, 5).reshape(-1)
    return np.eye(VOX, dtype=np.float32)[ids].reshape(8, 64, VOX)


def fill_columns(ids, look, pad, col, brick, flip):
    span = {-1: (slice(7, 8), slice(0, 1)), 0: (slice(0, 8), slice(1, 9)), 1: (slice(0, 1), slice(9, 10))}
    for offset in range(TAPS):
        sx, sy, sz = offset // 9 - 1, offset // 3 % 3 - 1, offset % 3 - 1
        n = ids[brick * TAPS + offset]
        low = 8 + 8 * sz
        pad[span[sx][1], span[sy][1], low : low + 8, :] = look[n, span[sx][0], span[sy][0], :, :]
    for b in range(3):
        for c in range(3):
            window = pad[:, b : b + 8, 7 + c : 15 + c, :].reshape(640, LANES).astype(jnp.bfloat16)
            for a in range(3):
                k = 9 * a + 3 * b + c
                k = TAPS - 1 - k if flip else k
                col[:, k * LANES : (k + 1) * LANES] = window[a * 64 : a * 64 + VOX]


def mm(a, b, da=1, db=0):
    return lax.dot_general(a, b, (((da,), (db,)), ((), ())), preferred_element_type=jnp.float32)


def forward_kernel(ids, look, live, w, wd, order, pre_ref, strided_ref, piece_ref, pad, col):
    brick = pl.program_id(0)
    fill_columns(ids, look, pad, col, brick, False)
    pre = mm(col[...], w[...]) * live[0]
    pre_ref[0] = pre
    hidden = (pre * jax.nn.sigmoid(pre)).astype(jnp.bfloat16)
    strided = mm(order[...], hidden).astype(jnp.bfloat16)
    strided_ref[0] = strided
    total = None
    for t in range(8):
        term = mm(wd[t], strided[t * 64 : (t + 1) * 64], 1, 1)
        total = term if total is None else total + term
    piece_ref[0] = total.astype(jnp.bfloat16)


def weight_kernel(ids, look, live, gp, pre, strided, wd, order, gpre_ref, sub_ref, down_ref, pad, col):
    brick = pl.program_id(0)

    @pl.when(brick == 0)
    def _():
        sub_ref[...] = jnp.zeros_like(sub_ref)
        down_ref[...] = jnp.zeros_like(down_ref)

    fill_columns(ids, look, pad, col, brick, False)
    piece = gp[0]
    terms = []
    for t in range(8):
        down_ref[t] += mm(piece, strided[0, t * 64 : (t + 1) * 64])
        terms.append(mm(piece, wd[t], 0, 0))
    split = jnp.concatenate(terms, axis=0)
    high = split.astype(jnp.bfloat16)
    rest = (split - high.astype(jnp.float32)).astype(jnp.bfloat16)
    hidden = mm(order[...], high, 0, 0) + mm(order[...], rest, 0, 0)
    grad = (hidden * silu_slope(pre[0]) * live[0]).astype(jnp.bfloat16)
    gpre_ref[0] = grad
    sub_ref[...] += mm(grad, col[...], 0, 0)


def feature_kernel(ids, look, live, w, out_ref, pad, col):
    brick = pl.program_id(0)
    fill_columns(ids, look, pad, col, brick, True)
    out_ref[0] = (mm(col[...], w[...]) * live[0]).astype(jnp.bfloat16)


def whole(shape):
    return pl.BlockSpec(shape, lambda b, ids: (0,) * len(shape), pipeline_mode=pl.Buffered(1))


def summed(shape):
    return pl.BlockSpec(shape, lambda b, ids: (0,) * len(shape))


def each(shape):
    return pl.BlockSpec((1,) + shape, lambda b, ids: (b,) + (0,) * len(shape))


def call(kernel, bricks, in_specs, out_specs, out_shape, flops):
    return pl.pallas_call(
        kernel,
        grid_spec=pltpu.PrefetchScalarGridSpec(
            num_scalar_prefetch=1,
            grid=(bricks,),
            in_specs=in_specs,
            out_specs=out_specs,
            scratch_shapes=[
                pltpu.VMEM((10, 10, 24, LANES), jnp.float32),
                pltpu.VMEM((VOX, TAPS * LANES), jnp.bfloat16),
            ],
        ),
        out_shape=out_shape,
        compiler_params=pltpu.CompilerParams(
            dimension_semantics=("arbitrary",), vmem_limit_bytes=VMEM_BYTES
        ),
        cost_estimate=pl.CostEstimate(flops=flops, bytes_accessed=40_000_000, transcendentals=0),
    )


def rim_lookup(own, pick):
    bricks, voxels, channels = own.shape
    x = jnp.einsum("eb,bvc->evc", pick, own, preferred_element_type=jnp.float32)
    x = x.astype(jnp.bfloat16)[None, None]
    for axis, dim in (("gx", 0), ("yz", 1)):
        size = lax.axis_size(axis)
        up = [(i, (i + 1) % size) for i in range(size - 1)]
        down = [(j, i) for i, j in up]
        before = lax.ppermute(x, axis, up)
        after = lax.ppermute(x, axis, down)
        x = jnp.concatenate([before, x, after], axis=dim)
    arrived = x.reshape(-1, voxels, channels)
    everything = jnp.concatenate([own, arrived], axis=0)
    everything = jnp.pad(everything, ((0, 1), (0, 0), (0, LANES - channels)))
    return everything.astype(jnp.float32).reshape(-1, EDGE, EDGE, EDGE, LANES)


def on_device(
    features, occupancy, neighbours, exports, coarse_map, owners, w_sub, w_down, cotangent
):
    bricks, channels, voxels = features.shape
    coarse_channels = w_down.shape[1]
    groups = lax.axis_size("yz")
    f32, bf16 = jnp.float32, jnp.bfloat16
    ids = neighbours.reshape(-1)
    live = occupancy.astype(f32)[:, :, None]
    pick = (exports[:, None] == jnp.arange(bricks)[None, :]).astype(bf16)
    own = (features * occupancy.astype(bf16)[:, None, :]).transpose(0, 2, 1)
    look = rim_lookup(own, pick)

    lanes_more = LANES - channels
    w_in = jnp.pad(w_sub.transpose(0, 2, 1), ((0, 0), (0, lanes_more), (0, 0))).reshape(-1, channels)
    w_out = jnp.pad(w_sub, ((0, 0), (0, lanes_more), (0, 0))).reshape(-1, channels)
    order = jnp.asarray(fine_order(), bf16)

    cell = coarse_map[:, 0]
    earlier = jnp.arange(bricks)[None, :] < jnp.arange(bricks)[:, None]
    rank = jnp.sum((cell[:, None] == cell[None, :]) & earlier, axis=1)
    owner = jnp.sum(jnp.where(cell[:, None] == jnp.arange(owners.shape[0])[None, :], owners[None, :], 0), axis=1)
    select = (
        (owner[None, None, :] == jnp.arange(groups)[:, None, None])
        & (rank[None, None, :] == jnp.arange(3)[None, :, None])
    ).astype(bf16)
    octant = (coarse_map[:, 1][:, None] == jnp.arange(8)[None, :]).astype(bf16)
    place = jnp.einsum("grb,bp->grp", select, octant, preferred_element_type=f32).astype(bf16)
    place = lax.all_to_all(place, "yz", split_axis=0, concat_axis=0, tiled=True)
    spread = jnp.einsum(
        "srp,puv->sruv", place, jnp.asarray(block_order(), bf16), preferred_element_type=f32
    ).astype(bf16)
    cot_piece = jnp.einsum("scv,sruv->srcu", cotangent, spread, preferred_element_type=f32)

    conv_flops = 2 * bricks * VOX * TAPS * LANES * channels
    look_shape = look.shape
    pre, strided, piece = call(
        forward_kernel,
        bricks,
        [
            whole(look_shape),
            each((voxels, 1)),
            whole(w_in.shape),
            whole(w_down.shape),
            whole(order.shape),
        ],
        [each((voxels, channels)), each((voxels, channels)), each((coarse_channels, 64))],
        [
            jax.ShapeDtypeStruct((bricks, voxels, channels), f32),
            jax.ShapeDtypeStruct((bricks, voxels, channels), bf16),
            jax.ShapeDtypeStruct((bricks, coarse_channels, 64), bf16),
        ],
        conv_flops,
    )(ids, look, live, w_in, w_down, order)

    outgoing = jnp.einsum("grb,bcu->grcu", select, piece, preferred_element_type=f32).astype(bf16)
    arrived = lax.all_to_all(outgoing, "yz", split_axis=0, concat_axis=0, tiled=True)
    slope = silu_slope(arrived.astype(f32))
    back = (cot_piece * slope).astype(bf16)
    returned = lax.all_to_all(back, "yz", split_axis=0, concat_axis=0, tiled=True)
    coarse_pre = jnp.einsum("srcu,sruv->scv", arrived, spread, preferred_element_type=f32)
    coarse = jax.nn.silu(coarse_pre).astype(bf16)
    grad_piece = jnp.einsum("grb,grcu->bcu", select, returned, preferred_element_type=f32).astype(bf16)

    grad_pre, sub_local, down_local = call(
        weight_kernel,
        bricks,
        [
            whole(look_shape),
            each((voxels, 1)),
            each((coarse_channels, 64)),
            each((voxels, channels)),
            each((voxels, channels)),
            whole(w_down.shape),
            whole(order.shape),
        ],
        [
            each((voxels, channels)),
            summed((channels, TAPS * LANES)),
            summed(w_down.shape),
        ],
        [
            jax.ShapeDtypeStruct((bricks, voxels, channels), bf16),
            jax.ShapeDtypeStruct((channels, TAPS * LANES), f32),
            jax.ShapeDtypeStruct(w_down.shape, f32),
        ],
        conv_flops,
    )(ids, look, live, grad_piece, pre, strided, w_down, order)

    sub_local = sub_local.reshape(channels, TAPS, LANES)[:, :, :channels].transpose(1, 0, 2)
    grad_sub, grad_down = lax.psum((sub_local, down_local), ("gx", "yz"))

    grad_look = rim_lookup(grad_pre, pick)
    grad_own = call(
        feature_kernel,
        bricks,
        [whole(look_shape), each((voxels, 1)), whole(w_out.shape)],
        each((voxels, channels)),
        jax.ShapeDtypeStruct((bricks, voxels, channels), bf16),
        conv_flops,
    )(ids, grad_look, live, w_out)
    return (coarse, grad_own.transpose(0, 2, 1), grad_sub, grad_down)


def solution(mesh):
    split = ("gx", "yz")
    in_specs = (
        P(split, None, None),
        P(split, None),
        P(split, None),
        P(split),
        P(split, None),
        P(split),
        P(),
        P(),
        P(split, None, None),
    )
    out_specs = (P(split, None, None), P(split, None, None), P(), P())
    return jax.shard_map(
        on_device, mesh=mesh, in_specs=in_specs, out_specs=out_specs, check_vma=False
    )
```

time: 815 us -> 506 us (0.62)
  matrix products: 260 us -> 10.5 us
  local copies, waits for them, and re-layouts: 183 us -> 85.7 us
  Pallas kernels: 0 us -> 96.7 us
  other arithmetic: 112 us -> 39.9 us
  blocking collectives: 55.4 us -> 15 us
  starting transfers between devices: 30.3 us -> 68.3 us
  waiting for transfers between devices: 149 us -> 173 us
    dot_general x86 -> x8, matrix products: 260 us -> 10.5 us  [the longest x1 4.53 us: on_device(): jnp.einsum('srcu,sruv->scv', arrived, spread, preferred_element_type=f32)]
    pallas_call x0 -> x3, Pallas kernels: none -> 96.7 us  [the longest x1 36.7 us: on_device(): call(weight_kernel, bricks, [whole(look_shape), each((voxels, 1)), each((...]
    gather x57 -> x0, local copies, waits for them, and re-layouts: 67.5 us -> none  [the longest x54 63.4 us: pad_bricks(): picked = jnp.take(facing, neighbour_ids[:, offset], axis=0)]
    all_to_all x1, blocking collectives: 55.4 us -> 15 us  [on_device(): lax.all_to_all(back, 'yz', split_axis=0, concat_axis=0, tiled=True)]
    all_to_all x1 -> x2, starting transfers between devices: 4.31 us -> 43.2 us  [the longest x1 39.3 us: on_device(): lax.all_to_all(outgoing, 'yz', split_axis=0, concat_axis=0, tiled=True)]
    scatter x52 -> x0, other arithmetic: 35.7 us -> none  [pad_bricks(): padded = padded.at[:, :, spans[0][1], spans[1][1], spans[2][1]].set(picked)]
    another operation x51 -> x0, local copies, waits for them, and re-layouts: 34.2 us -> none  [the longest x50 33.3 us: pad_bricks(): picked = jnp.take(facing, neighbour_ids[:, offset], axis=0)]
    ppermute x8, waiting for transfers between devices: 0.02 us -> 32.8 us  [the longest x4 30.5 us: rim_lookup(): after = lax.ppermute(x, axis, down)]
  transfers between devices with their start and end apart: 10 -> 11, of which waited for: 2 -> 6; matrix products, arithmetic and copies ran while one was open for 10% -> 14% of each run, Pallas kernels for 0% -> 7%
where the time goes in v1:
time: 506 us; the launch traced here: 504 us
  waiting for transfers between devices  173 us (34%)
  Pallas kernels  96.7 us (19%)
  local copies, waits for them, and re-layouts  85.7 us (17%)
  starting transfers between devices  68.3 us (13%)
  other arithmetic  39.9 us (8%)
  blocking collectives  15 us (3%)
  between operations  14.3 us (3%)
  matrix products  10.5 us (2%)
    psum x1, waiting for transfers between devices, on_device(): grad_sub, grad_down = lax.psum((sub_local, down_local), ('gx', 'yz'))  130 us
    reshape x2, local copies, waits for them, and re-layouts, rim_lookup(): return everything.astype(jnp.float32).reshape(-1, EDGE, EDGE, EDGE, LANES)  44.6 us
    all_to_all x1, starting transfers between devices, on_device(): lax.all_to_all(outgoing, 'yz', split_axis=0, concat_axis=0, tiled=True)  39.3 us
    pallas_call x1, Pallas kernels, on_device(): call(weight_kernel, bricks, [whole(look_shape), each((voxels, 1)), each((...  36.7 us
    pallas_call x1, Pallas kernels, on_device(): call(forward_kernel, bricks, [whole(look_shape), each((voxels, 1)), whole...  34 us
    ppermute x4, waiting for transfers between devices, rim_lookup(): after = lax.ppermute(x, axis, down)  30.5 us
    reshape x2, other arithmetic, rim_lookup(): return everything.astype(jnp.float32).reshape(-1, EDGE, EDGE, EDGE, LANES)  26.2 us
    pallas_call x1, Pallas kernels, on_device(): call(feature_kernel, bricks, [whole(look_shape), each((voxels, 1)), whole...  25.9 us
  transfers between devices with their start and end apart: 11, of which 6 were waited for; matrix products, arithmetic and copies ran while one was open for 14% of the time, Pallas kernels for 7%

profile of v1, /device:TPU:0, one launch (start us, length us, event | category | flops | bytes accessed | tf_op | source)
XLA Modules:
  0.0 503.7 jit_solution(6488331093820847962)
XLA Ops:
  7.2 1.5 convert_bitcast_fusion
  8.7 1.4 multiply_bitcast_fusion
  10.9 1.4 collective-permute-start.1
  12.3 5.6 %collective-permute-start = (bf16[1,1,8,512,96]{3,2,4,1,0:T(8,128)(2,1)S(1)}, bf16[1,1,8,512,96]{3,2,4,1,0:T(8,128)(2,1)S(1)}, u32[]{:S(2)}, u32[]{:S(2)}) collective-permute-start(bf16[1,1,8,512,96]{3,2,4,1,0:T(8,128)(2,1)S(1)} %fusion.36), channel_id=1, source_target_pairs={{0,8},{8,16},{16,24},{1,9},{9,17},{17,25},{2,10},{10,18},{18,26},{... | collective-permute-start | bytes 2359304 | tf_op jit(solution)/shard_map/ppermute | solution.py:136
  17.9 15.6 %collective-permute-done.1 = bf16[1,1,8,512,96]{3,2,4,1,0:T(8,128)(2,1)S(1)} collective-permute-done((bf16[1,1,8,512,96]{3,2,4,1,0:T(8,128)(2,1)S(1)}, bf16[1,1,8,512,96]{3,2,4,1,0:T(8,128)(2,1)S(1)}, u32[]{:S(2)}, u32[]{:S(2)}) %collective-permute-start.1) | collective-permute-done | bytes 786464 | tf_op jit(solution)/shard_map/ppermute | solution.py:137
  33.5 1.2 collective-permute-done
  34.6 1.7 pad_maximum_fusion.2
  36.4 1.3 collective-permute-start.3
  37.6 4.5 collective-permute-start.2
  43.1 3.9 all-to-all-start.1
  47.0 1.4 reshape.86.ids
  48.4 3.0 copy.90.live
  51.4 2.2 copy.115
  53.5 2.2 pad.15.clone
  55.8 3.8 pad_maximum_fusion
  59.5 5.6 %copy.87 = bf16[3,3,8,512,96]{3,4,2,1,0:T(8,128)(2,1)} copy(bf16[3,3,8,512,96]{3,2,4,1,0:T(8,128)(2,1)S(1)} %pad_maximum_fusion) | data formatting | bytes 14155776 | tf_op jit(solution)/shard_map/concatenate | solution.py:138
  65.1 13.1 %fusion.7 = f32[85,512,128]{1,2,0:T(8,128)} fusion(bf16[72,512,96]{1,2,0:T(8,128)(2,1)} %bitcast.73, bf16[12,512,96]{1,2,0:T(8,128)(2,1)S(1)} %multiply_bitcast_fusion), kind=kLoop, calls=%fused_computation.9 | loop fusion | flops 61276160 | bytes 30539776 | tf_op jit(solution)/shard_map/reshape | solution.py:142
  78.2 22.3 %copy.88 = f32[85,512,128]{2,1,0:T(8,128)} copy(f32[85,512,128]{1,2,0:T(8,128)} %fusion.7) | data formatting | bytes 44564480 | tf_op jit(solution)/shard_map/reshape | solution.py:142
  100.5 34.0 %shard_map.138 = (f32[12,512,96]{2,1,0:T(8,128)}, bf16[12,512,96]{2,1,0:T(8,128)(2,1)}, bf16[12,192,64]{2,1,0:T(8,128)(2,1)}) custom-call(s32[324]{0:T(512)} %reshape.86.ids, f32[85,8,8,8,128]{4,3,2,1,0:T(8,128)} %bitcast.70, f32[12,512,1]{2,1,0:T(8,128)} %copy.90.live, bf16[3456,96]{1,0:T(8,128)(2,1)} %bitcast.77, bf16[8,192,96]{2,1,0:T(8,128)(2,1)} %wd.3, ...), custom_call_target="tpu_custom_call" | custom-call | flops 4076863488 | bytes 40000000 | tf_op jit(solution)/shard_map/pallas_call | solution.py:181
  134.6 1.8 copy.91
  137.8 39.3 %all-to-all-start = ((bf16[8,3,192,64]{2,3,1,0:T(8,128)(2,1)}), bf16[8,3,192,64]{2,3,1,0:T(8,128)(2,1)}, u32[]{:S(2)}, u32[]{:S(2)}) async-start(bf16[8,3,192,64]{2,3,1,0:T(8,128)(2,1)} %copy.92), calls=%async_computation | async-start | bytes 1572864 | tf_op jit(solution)/shard_map/all_to_all | solution.py:201
  177.3 1.6 convolution_convert_fusion
  178.9 10.9 %all-to-all-done = bf16[8,3,192,64]{2,3,1,0:T(8,128)(2,1)} async-done(((bf16[8,3,192,64]{2,3,1,0:T(8,128)(2,1)}), bf16[8,3,192,64]{2,3,1,0:T(8,128)(2,1)}, u32[]{:S(2)}, u32[]{:S(2)}) %all-to-all-start) | async-done | bytes 589856 | tf_op jit(solution)/shard_map/all_to_all | solution.py:201
  189.8 2.2 fusion.23
  192.0 15.0 %all_to_all.15 = bf16[8,3,192,64]{2,3,1,0:T(8,128)(2,1)S(1)} all-to-all(bf16[8,3,192,64]{2,3,1,0:T(8,128)(2,1)S(1)} %fusion.23), channel_id=1, replica_groups=mesh['gx'=4,'yz'=8] {'yz'}, dimensions={0} | all-to-all | bytes 1179648 | tf_op jit(solution)/shard_map/all_to_all | solution.py:204
  208.7 36.7 %shard_map.139 = (bf16[12,512,96]{2,1,0:T(8,128)(2,1)}, f32[96,3456]{1,0:T(8,128)}, f32[8,192,96]{2,1,0:T(8,128)}) custom-call(s32[324]{0:T(512)} %reshape.86.ids, f32[85,8,8,8,128]{4,3,2,1,0:T(8,128)} %bitcast.71, f32[12,512,1]{2,1,0:T(8,128)} %copy.90.live, bf16[12,192,64]{2,1,0:T(8,128)(2,1)} %copy.100.gp, f32[12,512,96]{2,1,0:T(8,128)} %get-tuple-element.11.pre, ...), custom_call_target="tpu_custom_call" | custom-call | flops 4076863488 | bytes 40000000 | tf_op jit(solution)/shard_map/pallas_call | solution.py:209
  245.5 3.4 copy.101
  249.3 1.3 collective-permute-start.5
  250.6 5.1 %collective-permute-start.4 = (bf16[1,1,8,512,96]{3,2,4,1,0:T(8,128)(2,1)S(1)}, bf16[1,1,8,512,96]{3,2,4,1,0:T(8,128)(2,1)S(1)}, u32[]{:S(2)}, u32[]{:S(2)}) collective-permute-start(bf16[1,1,8,512,96]{3,2,4,1,0:T(8,128)(2,1)S(1)} %fusion.35), channel_id=1, source_target_pairs={{0,8},{8,16},{16,24},{1,9},{9,17},{17,25},{2,10},{10,18},{18,26},{... | collective-permute-start | bytes 2359304 | tf_op jit(solution)/shard_map/ppermute | solution.py:136
  255.7 14.9 %collective-permute-done.5 = bf16[1,1,8,512,96]{3,2,4,1,0:T(8,128)(2,1)S(1)} collective-permute-done((bf16[1,1,8,512,96]{3,2,4,1,0:T(8,128)(2,1)S(1)}, bf16[1,1,8,512,96]{3,2,4,1,0:T(8,128)(2,1)S(1)}, u32[]{:S(2)}, u32[]{:S(2)}) %collective-permute-start.5) | collective-permute-done | bytes 786464 | tf_op jit(solution)/shard_map/ppermute | solution.py:137
  270.6 1.2 collective-permute-done.4
  271.7 1.7 pad_maximum_fusion.3
  273.4 1.3 collective-permute-start.7
  274.7 4.5 collective-permute-start.6
  279.2 1.5 reshape.95
  280.7 1.3 slice_bitcast_fusion
  282.0 1.1 copy-done.8
  283.1 1.2 pad.17
  284.2 4.5 fusion.16
  288.8 1.5 copy.103
  290.2 129.6 %all-reduce.7.cloned.1.call-done = (f32[27,96,96]{2,0,1:T(8,128)}, f32[8,192,96]{2,1,0:T(8,128)}) async-done(((f32[27,96,96]{2,0,1:T(8,128)}, f32[8,192,96]{2,1,0:T(8,128)}), (f32[27,96,96]{2,0,1:T(8,128)}, f32[8,192,96]{2,1,0:T(8,128)})) %all-reduce.7.cloned.1.call-update) | async-done | bytes 1585168 | tf_op jit(solution)/shard_map/psum | solution.py:235
  419.9 3.2 copy.107
  423.1 3.4 pad_maximum_fusion.1
  426.5 5.6 %copy.102 = bf16[3,3,8,512,96]{3,4,2,1,0:T(8,128)(2,1)} copy(bf16[3,3,8,512,96]{3,2,4,1,0:T(8,128)(2,1)S(1)} %pad_maximum_fusion.1) | data formatting | bytes 14155776 | tf_op jit(solution)/shard_map/concatenate | solution.py:138
  432.1 13.1 %fusion.12 = f32[85,512,128]{1,2,0:T(8,128)} fusion(bf16[72,512,96]{1,2,0:T(8,128)(2,1)} %bitcast.74, bf16[12,512,96]{1,2,0:T(8,128)(2,1)S(1)} %copy-done.3), kind=kLoop, calls=%fused_computation.14 | loop fusion | flops 61276160 | bytes 30539776 | tf_op jit(solution)/shard_map/reshape | solution.py:142
  445.2 22.3 %copy.104 = f32[85,512,128]{2,1,0:T(8,128)} copy(f32[85,512,128]{1,2,0:T(8,128)} %fusion.12) | data formatting | bytes 44564480 | tf_op jit(solution)/shard_map/reshape | solution.py:142
  467.5 25.9 %shard_map.140 = bf16[12,512,96]{2,1,0:T(8,128)(2,1)} custom-call(s32[324]{0:T(512)} %reshape.86.ids, f32[85,8,8,8,128]{4,3,2,1,0:T(8,128)} %bitcast.72, f32[12,512,1]{2,1,0:T(8,128)} %copy.90.live, bf16[3456,96]{1,0:T(8,128)(2,1)} %bitcast.76), custom_call_target="tpu_custom_call" | custom-call | flops 4076863488 | bytes 40000000 | tf_op jit(solution)/shard_map/pallas_call | solution.py:238
  493.4 2.6 copy.106
  (51 shorter events, 6.5 us)
Async XLA Ops:
  7.2 182.6 %copy-start = (bf16[8,192,512]{2,1,0:T(8,128)(2,1)S(1)}, bf16[8,192,512]{2,1,0:T(8,128)(2,1)}, u32[]{:S(2)}) copy-start(bf16[8,192,512]{2,1,0:T(8,128)(2,1)} %param.19) | copy-start | bytes 4718596
  7.2 2.9 copy-start.11
  10.8 31.3 %copy-start.13 = (s32[12,2]{0,1:T(2,128)S(1)}, s32[12,2]{0,1:T(2,128)}, u32[]{:S(2)}) copy-start(s32[12,2]{0,1:T(2,128)} %param.15) | copy-start | bytes 292
  10.9 31.4 %copy-start.14 = (s32[4]{0:T(128)S(1)}, s32[4]{0:T(128)}, u32[]{:S(2)}) copy-start(s32[4]{0:T(128)} %param.16) | copy-start | bytes 52
  10.9 22.6 %collective-permute-start.1 = (bf16[1,1,8,512,96]{3,2,4,1,0:T(8,128)(2,1)S(1)}, bf16[1,1,8,512,96]{3,2,4,1,0:T(8,128)(2,1)S(1)}, u32[]{:S(2)}, u32[]{:S(2)}) collective-permute-start(bf16[1,1,8,512,96]{3,2,4,1,0:T(8,128)(2,1)S(1)} %fusion.36), channel_id=1, source_target_pairs={{8,0},{16,8},{24,16},{9,1},{17,9},{25,17},{10,2},{18,10},{26,18},{... | collective-permute-start | bytes 2359304 | tf_op jit(solution)/shard_map/ppermute | solution.py:137
  12.3 22.3 %collective-permute-start = (bf16[1,1,8,512,96]{3,2,4,1,0:T(8,128)(2,1)S(1)}, bf16[1,1,8,512,96]{3,2,4,1,0:T(8,128)(2,1)S(1)}, u32[]{:S(2)}, u32[]{:S(2)}) collective-permute-start(bf16[1,1,8,512,96]{3,2,4,1,0:T(8,128)(2,1)S(1)} %fusion.36), channel_id=1, source_target_pairs={{0,8},{8,16},{16,24},{1,9},{9,17},{17,25},{2,10},{10,18},{18,26},{... | collective-permute-start | bytes 2359304 | tf_op jit(solution)/shard_map/ppermute | solution.py:136
  33.5 2.9 copy-start.6
  34.6 1.7 copy-start.7
  36.4 19.4 %collective-permute-start.3 = (bf16[3,1,8,512,96]{3,2,4,1,0:T(8,128)(2,1)}, bf16[3,1,8,512,96]{3,2,4,1,0:T(8,128)(2,1)}, u32[]{:S(2)}, u32[]{:S(2)}) collective-permute-start(bf16[3,1,8,512,96]{3,2,4,1,0:T(8,128)(2,1)} %pad_maximum_fusion.2), channel_id=1, source_target_pairs={{1,0},{2,1},{3,2},{4,3},{5,4},{6,5},{7,6},{9,8},{10,9},{11,10},{12... | collective-permute-start | bytes 7077896 | tf_op jit(solution)/shard_map/ppermute | solution.py:137
  37.6 18.1 %collective-permute-start.2 = (bf16[3,1,8,512,96]{3,2,4,1,0:T(8,128)(2,1)}, bf16[3,1,8,512,96]{3,2,4,1,0:T(8,128)(2,1)}, u32[]{:S(2)}, u32[]{:S(2)}) collective-permute-start(bf16[3,1,8,512,96]{3,2,4,1,0:T(8,128)(2,1)} %pad_maximum_fusion.2), channel_id=1, source_target_pairs={{0,1},{1,2},{2,3},{3,4},{4,5},{5,6},{6,7},{8,9},{9,10},{10,11},{11... | collective-permute-start | bytes 7077896 | tf_op jit(solution)/shard_map/ppermute | solution.py:136
  43.1 94.6 %all-to-all-start.1 = ((bf16[8,3,8]{2,1,0:T(4,128)(2,1)}), bf16[8,3,8]{2,1,0:T(4,128)(2,1)S(1)}, u32[]{:S(2)}, u32[]{:S(2)}) async-start(bf16[8,3,8]{2,1,0:T(4,128)(2,1)} %copy.93), calls=%async_computation.1 | async-start | bytes 16384 | tf_op jit(solution)/shard_map/all_to_all | solution.py:173
  137.8 52.1 %all-to-all-start = ((bf16[8,3,192,64]{2,3,1,0:T(8,128)(2,1)}), bf16[8,3,192,64]{2,3,1,0:T(8,128)(2,1)}, u32[]{:S(2)}, u32[]{:S(2)}) async-start(bf16[8,3,192,64]{2,3,1,0:T(8,128)(2,1)} %copy.92), calls=%async_computation | async-start | bytes 1572864 | tf_op jit(solution)/shard_map/all_to_all | solution.py:201
  177.1 242.8 %all-reduce.7.cloned.1.call-start = ((), (), s32[]{:S(2)}) async-start(), calls=%async_computation.3 | async-start | bytes 4718592 | tf_op jit(solution)/shard_map/psum | solution.py:235
  178.9 13.1 %copy-start.9 = (bf16[8,3,64,512]{3,0,2,1:T(8,128)(2,1)}, bf16[8,3,64,512]{3,0,2,1:T(8,128)(2,1)S(1)}, u32[]{:S(2)}) copy-start(bf16[8,3,64,512]{3,0,2,1:T(8,128)(2,1)S(1)} %convolution_convert_fusion) | copy-start | bytes 4718596
  245.5 3.4 copy-start.12
  249.3 21.3 %collective-permute-start.5 = (bf16[1,1,8,512,96]{3,2,4,1,0:T(8,128)(2,1)S(1)}, bf16[1,1,8,512,96]{3,2,4,1,0:T(8,128)(2,1)S(1)}, u32[]{:S(2)}, u32[]{:S(2)}) collective-permute-start(bf16[1,1,8,512,96]{3,2,4,1,0:T(8,128)(2,1)S(1)} %fusion.35), channel_id=1, source_target_pairs={{8,0},{16,8},{24,16},{9,1},{17,9},{25,17},{10,2},{18,10},{26,18},{... | collective-permute-start | bytes 2359304 | tf_op jit(solution)/shard_map/ppermute | solution.py:137
  250.6 21.2 %collective-permute-start.4 = (bf16[1,1,8,512,96]{3,2,4,1,0:T(8,128)(2,1)S(1)}, bf16[1,1,8,512,96]{3,2,4,1,0:T(8,128)(2,1)S(1)}, u32[]{:S(2)}, u32[]{:S(2)}) collective-permute-start(bf16[1,1,8,512,96]{3,2,4,1,0:T(8,128)(2,1)S(1)} %fusion.35), channel_id=1, source_target_pairs={{0,8},{8,16},{16,24},{1,9},{9,17},{17,25},{2,10},{10,18},{18,26},{... | collective-permute-start | bytes 2359304 | tf_op jit(solution)/shard_map/ppermute | solution.py:136
  271.7 1.7 copy-start.4
  273.4 149.7 %collective-permute-start.7 = (bf16[3,1,8,512,96]{3,2,4,1,0:T(8,128)(2,1)}, bf16[3,1,8,512,96]{3,2,4,1,0:T(8,128)(2,1)}, u32[]{:S(2)}, u32[]{:S(2)}) collective-permute-start(bf16[3,1,8,512,96]{3,2,4,1,0:T(8,128)(2,1)} %pad_maximum_fusion.3), channel_id=1, source_target_pairs={{1,0},{2,1},{3,2},{4,3},{5,4},{6,5},{7,6},{9,8},{10,9},{11,10},{12... | collective-permute-start | bytes 7077896 | tf_op jit(solution)/shard_map/ppermute | solution.py:137
  274.7 148.4 %collective-permute-start.6 = (bf16[3,1,8,512,96]{3,2,4,1,0:T(8,128)(2,1)}, bf16[3,1,8,512,96]{3,2,4,1,0:T(8,128)(2,1)}, u32[]{:S(2)}, u32[]{:S(2)}) collective-permute-start(bf16[3,1,8,512,96]{3,2,4,1,0:T(8,128)(2,1)} %pad_maximum_fusion.3), channel_id=1, source_target_pairs={{0,1},{1,2},{2,3},{3,4},{4,5},{5,6},{6,7},{8,9},{9,10},{10,11},{11... | collective-permute-start | bytes 7077896 | tf_op jit(solution)/shard_map/ppermute | solution.py:136
  282.0 1.1 copy-start.8
  284.2 4.5 copy-start.2
  290.2 132.9 %copy-start.5 = (bf16[1,1,8,512,96]{3,2,4,1,0:T(8,128)(2,1)S(1)}, bf16[1,1,8,512,96]{3,2,4,1,0:T(8,128)(2,1)}, u32[]{:S(2)}) copy-start(bf16[1,1,8,512,96]{3,2,4,1,0:T(8,128)(2,1)} %copy-done.4) | copy-start | bytes 2359300
  426.5 5.6 %copy-start.3 = (bf16[12,512,96]{1,2,0:T(8,128)(2,1)S(1)}, bf16[12,512,96]{1,2,0:T(8,128)(2,1)}, u32[]{:S(2)}) copy-start(bf16[12,512,96]{1,2,0:T(8,128)(2,1)} %copy.103) | copy-start | bytes 3538948
  467.5 29.4 %copy-start.1 = (bf16[8,192,512]{2,1,0:T(8,128)(2,1)S(1)}, bf16[8,192,512]{2,1,0:T(8,128)(2,1)}, u32[]{:S(2)}) copy-start(bf16[8,192,512]{2,1,0:T(8,128)(2,1)} %param.19) | copy-start | bytes 4718596
  493.4 2.6 copy-start.10
Sparse Core Ops, SparseCore 0:
  282.1 137.6 all-reduce.6

commit v2 on v1

--- a/solution.py
+++ b/solution.py
@@ -26,6 +26,26 @@
 def block_order():
     ids = np.arange(VOX).reshape(2, 4, 2, 4, 2, 4).transpose(0, 2, 4, 1, 3, 5).reshape(-1)
     return np.eye(VOX, dtype=np.float32)[ids].reshape(8, 64, VOX)
+
+
+def widen(own, arrived, look):
+    bricks, channels = own.shape[0], own.shape[2]
+
+    @pl.when(pl.program_id(0) == 0)
+    def _():
+        def put(source, first):
+            def body(n, carry):
+                block = source[n].astype(jnp.float32)
+                rest = jnp.zeros((block.shape[0], LANES - channels), jnp.float32)
+                look[first + n] = jnp.concatenate([block, rest], axis=1).reshape(EDGE, EDGE, EDGE, LANES)
+                return carry
+
+            lax.fori_loop(0, source.shape[0], body, 0)
+
+        put(own, 0)
+        put(arrived, bricks)
+        last = bricks + arrived.shape[0]
+        look[last] = jnp.zeros((EDGE, EDGE, EDGE, LANES), jnp.float32)
 
 
 def fill_columns(ids, look, pad, col, brick, flip):
@@ -48,8 +68,9 @@
     return lax.dot_general(a, b, (((da,), (db,)), ((), ())), preferred_element_type=jnp.float32)
 
 
-def forward_kernel(ids, look, live, w, wd, order, pre_ref, strided_ref, piece_ref, pad, col):
+def forward_kernel(ids, own, arrived, live, w, wd, order, pre_ref, strided_ref, piece_ref, look, pad, col):
     brick = pl.program_id(0)
+    widen(own, arrived, look)
     fill_columns(ids, look, pad, col, brick, False)
     pre = mm(col[...], w[...]) * live[0]
     pre_ref[0] = pre
@@ -63,7 +84,7 @@
     piece_ref[0] = total.astype(jnp.bfloat16)
 
 
-def weight_kernel(ids, look, live, gp, pre, strided, wd, order, gpre_ref, sub_ref, down_ref, pad, col):
+def weight_kernel(ids, own, arrived, live, gp, pre, strided, wd, order, gpre_ref, sub_ref, down_ref, look, pad, col):
     brick = pl.program_id(0)
 
     @pl.when(brick == 0)
@@ -71,6 +92,7 @@
         sub_ref[...] = jnp.zeros_like(sub_ref)
         down_ref[...] = jnp.zeros_like(down_ref)
 
+    widen(own, arrived, look)
     fill_columns(ids, look, pad, col, brick, False)
     piece = gp[0]
     terms = []
@@ -86,8 +108,9 @@
     sub_ref[...] += mm(grad, col[...], 0, 0)
 
 
-def feature_kernel(ids, look, live, w, out_ref, pad, col):
+def feature_kernel(ids, own, arrived, live, w, out_ref, look, pad, col):
     brick = pl.program_id(0)
+    widen(own, arrived, look)
     fill_columns(ids, look, pad, col, brick, True)
     out_ref[0] = (mm(col[...], w[...]) * live[0]).astype(jnp.bfloat16)
 
@@ -104,7 +127,7 @@
     return pl.BlockSpec((1,) + shape, lambda b, ids: (b,) + (0,) * len(shape))
 
 
-def call(kernel, bricks, in_specs, out_specs, out_shape, flops):
+def call(kernel, bricks, held, in_specs, out_specs, out_shape, flops):
     return pl.pallas_call(
         kernel,
         grid_spec=pltpu.PrefetchScalarGridSpec(
@@ -113,6 +136,7 @@
             in_specs=in_specs,
             out_specs=out_specs,
             scratch_shapes=[
+                pltpu.VMEM((held, EDGE, EDGE, EDGE, LANES), jnp.float32),
                 pltpu.VMEM((10, 10, 24, LANES), jnp.float32),
                 pltpu.VMEM((VOX, TAPS * LANES), jnp.bfloat16),
             ],
@@ -121,7 +145,7 @@
         compiler_params=pltpu.CompilerParams(
             dimension_semantics=("arbitrary",), vmem_limit_bytes=VMEM_BYTES
         ),
-        cost_estimate=pl.CostEstimate(flops=flops, bytes_accessed=40_000_000, transcendentals=0),
+        cost_estimate=pl.CostEstimate(flops=flops, bytes_accessed=100_000_000, transcendentals=0),
     )
 
 
@@ -136,10 +160,7 @@
         before = lax.ppermute(x, axis, up)
         after = lax.ppermute(x, axis, down)
         x = jnp.concatenate([before, x, after], axis=dim)
-    arrived = x.reshape(-1, voxels, channels)
-    everything = jnp.concatenate([own, arrived], axis=0)
-    everything = jnp.pad(everything, ((0, 1), (0, 0), (0, LANES - channels)))
-    return everything.astype(jnp.float32).reshape(-1, EDGE, EDGE, EDGE, LANES)
+    return x.reshape(-1, voxels, channels)
 
 
 def on_device(
@@ -153,7 +174,8 @@
     live = occupancy.astype(f32)[:, :, None]
     pick = (exports[:, None] == jnp.arange(bricks)[None, :]).astype(bf16)
     own = (features * occupancy.astype(bf16)[:, None, :]).transpose(0, 2, 1)
-    look = rim_lookup(own, pick)
+    around = rim_lookup(own, pick)
+    held = bricks + around.shape[0] + 1
 
     lanes_more = LANES - channels
     w_in = jnp.pad(w_sub.transpose(0, 2, 1), ((0, 0), (0, lanes_more), (0, 0))).reshape(-1, channels)
@@ -177,12 +199,12 @@
     cot_piece = jnp.einsum("scv,sruv->srcu", cotangent, spread, preferred_element_type=f32)
 
     conv_flops = 2 * bricks * VOX * TAPS * LANES * channels
-    look_shape = look.shape
     pre, strided, piece = call(
         forward_kernel,
         bricks,
-        [
-            whole(look_shape),
+        held,
+        [
+            whole(own.shape), whole(around.shape),
             each((voxels, 1)),
             whole(w_in.shape),
             whole(w_down.shape),
@@ -195,7 +217,7 @@
             jax.ShapeDtypeStruct((bricks, coarse_channels, 64), bf16),
         ],
         conv_flops,
-    )(ids, look, live, w_in, w_down, order)
+    )(ids, own, around, live, w_in, w_down, order)
 
     outgoing = jnp.einsum("grb,bcu->grcu", select, piece, preferred_element_type=f32).astype(bf16)
     arrived = lax.all_to_all(outgoing, "yz", split_axis=0, concat_axis=0, tiled=True)
@@ -209,8 +231,9 @@
     grad_pre, sub_local, down_local = call(
         weight_kernel,
         bricks,
-        [
-            whole(look_shape),
+        held,
+        [
+            whole(own.shape), whole(around.shape),
             each((voxels, 1)),
             each((coarse_channels, 64)),
             each((voxels, channels)),
@@ -229,20 +252,21 @@
             jax.ShapeDtypeStruct(w_down.shape, f32),
         ],
         conv_flops,
-    )(ids, look, live, grad_piece, pre, strided, w_down, order)
+    )(ids, own, around, live, grad_piece, pre, strided, w_down, order)
 
     sub_local = sub_local.reshape(channels, TAPS, LANES)[:, :, :channels].transpose(1, 0, 2)
     grad_sub, grad_down = lax.psum((sub_local, down_local), ("gx", "yz"))
 
-    grad_look = rim_lookup(grad_pre, pick)
+    grad_around = rim_lookup(grad_pre, pick)
     grad_own = call(
         feature_kernel,
         bricks,
-        [whole(look_shape), each((voxels, 1)), whole(w_out.shape)],
+        held,
+        [whole(own.shape), whole(around.shape), each((voxels, 1)), whole(w_out.shape)],
         each((voxels, channels)),
         jax.ShapeDtypeStruct((bricks, voxels, channels), bf16),
         conv_flops,
-    )(ids, grad_look, live, w_out)
+    )(ids, grad_pre, grad_around, live, w_out)
     return (coarse, grad_own.transpose(0, 2, 1), grad_sub, grad_down)
 
 

time: 506 us -> 453 us (0.90)
  local copies, waits for them, and re-layouts: 85.7 us -> 56.4 us
  other arithmetic: 39.9 us -> 17.5 us
    reshape x2 -> x0, local copies, waits for them, and re-layouts: 44.6 us -> none  [rim_lookup(): return everything.astype(jnp.float32).reshape(-1, EDGE, EDGE, EDGE, LANES)]
    reshape x2 -> x0, other arithmetic: 26.2 us -> none  [rim_lookup(): return everything.astype(jnp.float32).reshape(-1, EDGE, EDGE, EDGE, LANES)]
    concatenate x2, local copies, waits for them, and re-layouts: 11.2 us -> 23.4 us  [rim_lookup(): x = jnp.concatenate([before, x, after], axis=dim)]
    unnamed x34 -> x39, local copies, waits for them, and re-layouts: 10 us -> 12.8 us
  transfers between devices with their start and end apart: 11 -> 11, of which waited for: 6 -> 6; matrix products, arithmetic and copies ran while one was open for 14% -> 9% of each run, Pallas kernels for 7% -> 7%
where the time goes in v2:
time: 453 us; the launch traced here: 451 us
  waiting for transfers between devices  175 us (39%)
  Pallas kernels  92.2 us (20%)
  starting transfers between devices  69.5 us (15%)
  local copies, waits for them, and re-layouts  56.4 us (12%)
  other arithmetic  17.5 us (4%)
  blocking collectives  15 us (3%)
  between operations  14.3 us (3%)
  matrix products  11.5 us (3%)
    psum x1, waiting for transfers between devices, on_device(): grad_sub, grad_down = lax.psum((sub_local, down_local), ('gx', 'yz'))  131 us
    all_to_all x1, starting transfers between devices, on_device(): lax.all_to_all(outgoing, 'yz', split_axis=0, concat_axis=0, tiled=True)  40.7 us
    pallas_call x1, Pallas kernels, on_device(): call(weight_kernel, bricks, held, [whole(own.shape), whole(around.shape),...  35.3 us
    pallas_call x1, Pallas kernels, on_device(): call(forward_kernel, bricks, held, [whole(own.shape), whole(around.shape)...  32.5 us
    ppermute x4, waiting for transfers between devices, rim_lookup(): after = lax.ppermute(x, axis, down)  30.5 us
    pallas_call x1, Pallas kernels, on_device(): call(feature_kernel, bricks, held, [whole(own.shape), whole(around.shape)...  24.4 us
    concatenate x2, local copies, waits for them, and re-layouts, rim_lookup(): x = jnp.concatenate([before, x, after], axis=dim)  23.4 us
    ppermute x4, starting transfers between devices, rim_lookup(): before = lax.ppermute(x, axis, up)  19.6 us
  transfers between devices with their start and end apart: 11, of which 6 were waited for; matrix products, arithmetic and copies ran while one was open for 9% of the time, Pallas kernels for 7%

profile of v2, /device:TPU:0, one launch (start us, length us, event | category | flops | bytes accessed | tf_op | source)
XLA Modules:
  0.0 451.2 jit_solution(13307420224629376125)
XLA Ops:
  7.2 2.6 copy.82
  9.8 2.1 multiply_bitcast_fusion.own
  12.0 3.1 copy.83
  15.1 1.8 fusion.17
  17.0 1.4 collective-permute-start.1
  18.4 5.6 %collective-permute-start = (bf16[1,1,8,512,96]{3,2,4,1,0:T(8,128)(2,1)S(1)}, bf16[1,1,8,512,96]{3,2,4,1,0:T(8,128)(2,1)S(1)}, u32[]{:S(2)}, u32[]{:S(2)}) collective-permute-start(bf16[1,1,8,512,96]{3,2,4,1,0:T(8,128)(2,1)S(1)} %fusion.17), channel_id=1, source_target_pairs={{0,8},{8,16},{16,24},{1,9},{9,17},{17,25},{2,10},{10,18},{18,26},{... | collective-permute-start | bytes 2359304 | tf_op jit(solution)/shard_map/ppermute | solution.py:160
  24.0 15.6 %collective-permute-done.1 = bf16[1,1,8,512,96]{3,2,4,1,0:T(8,128)(2,1)S(1)} collective-permute-done((bf16[1,1,8,512,96]{3,2,4,1,0:T(8,128)(2,1)S(1)}, bf16[1,1,8,512,96]{3,2,4,1,0:T(8,128)(2,1)S(1)}, u32[]{:S(2)}, u32[]{:S(2)}) %collective-permute-start.1) | collective-permute-done | bytes 786464 | tf_op jit(solution)/shard_map/ppermute | solution.py:161
  39.6 1.2 collective-permute-done
  40.8 1.7 pad_maximum_fusion.2
  42.5 1.3 collective-permute-start.3
  43.8 4.5 collective-permute-start.2
  49.3 3.9 all-to-all-start.1
  53.1 0.7 reshape.76.ids
  53.8 2.2 copy.86.live
  56.0 2.3 copy.109
  58.2 2.3 pad.7.clone
  60.6 5.9 %pad_maximum_fusion = bf16[3,3,8,512,96]{3,2,4,1,0:T(8,128)(2,1)} fusion(bf16[3,1,8,512,96]{3,2,4,1,0:T(8,128)(2,1)} %collective-permute-done.3, bf16[1,1,8,512,96]{3,2,4,1,0:T(8,128)(2,1)S(1)} %collective-permute-done.1, bf16[1,1,8,512,96]{3,2,4,1,0:T(8,128)(2,1)S(1)} %copy-done.4, bf16[1,1,8,512,96]{3,2,4,1,0:T(8,128)(2,1)S(1)} %copy-done.8, ...), kind=kLoop, calls=%fused_computation | loop fusion | flops 14155776 | bytes 14155776 | tf_op jit(solution)/shard_map/concatenate | solution.py:162
  66.4 11.7 %copy.84 = bf16[3,3,8,512,96]{4,3,2,1,0:T(8,128)(2,1)} copy(bf16[3,3,8,512,96]{3,2,4,1,0:T(8,128)(2,1)} %pad_maximum_fusion) | data formatting | bytes 14155776 | tf_op jit(solution)/shard_map/concatenate | solution.py:162
  78.1 32.5 %shard_map.138 = (f32[12,512,96]{2,1,0:T(8,128)}, bf16[12,512,96]{2,1,0:T(8,128)(2,1)}, bf16[12,192,64]{2,1,0:T(8,128)(2,1)}) custom-call(s32[324]{0:T(512)} %reshape.76.ids, bf16[12,512,96]{2,1,0:T(8,128)(2,1)} %copy-done.2, bf16[72,512,96]{2,1,0:T(8,128)(2,1)} %bitcast.69, f32[12,512,1]{2,1,0:T(8,128)} %copy.86.live, bf16[3456,96]{1,0:T(8,128)(2,1)} %bitcast.74, ...), custom_call_target="tpu_custom_call" | custom-call | flops 4076863488 | bytes 100000000 | tf_op jit(solution)/shard_map/pallas_call | solution.py:202
  110.6 1.8 copy.87
  112.8 1.1 copy.88
  113.8 40.7 %all-to-all-start = ((bf16[8,3,192,64]{2,3,1,0:T(8,128)(2,1)}), bf16[8,3,192,64]{2,3,1,0:T(8,128)(2,1)}, u32[]{:S(2)}, u32[]{:S(2)}) async-start(bf16[8,3,192,64]{2,3,1,0:T(8,128)(2,1)} %copy.88), calls=%async_computation | async-start | bytes 1572864 | tf_op jit(solution)/shard_map/all_to_all | solution.py:223
  154.5 1.6 convolution_convert_fusion
  156.1 11.1 %all-to-all-done = bf16[8,3,192,64]{2,3,1,0:T(8,128)(2,1)} async-done(((bf16[8,3,192,64]{2,3,1,0:T(8,128)(2,1)}), bf16[8,3,192,64]{2,3,1,0:T(8,128)(2,1)}, u32[]{:S(2)}, u32[]{:S(2)}) %all-to-all-start) | async-done | bytes 589856 | tf_op jit(solution)/shard_map/all_to_all | solution.py:223
  167.2 2.2 fusion.10
  169.4 15.0 %all_to_all.15 = bf16[8,3,192,64]{2,3,1,0:T(8,128)(2,1)S(1)} all-to-all(bf16[8,3,192,64]{2,3,1,0:T(8,128)(2,1)S(1)} %fusion.10), channel_id=1, replica_groups=mesh['gx'=4,'yz'=8] {'yz'}, dimensions={0} | all-to-all | bytes 1179648 | tf_op jit(solution)/shard_map/all_to_all | solution.py:226
  185.1 1.0 copy.96.gp
  186.1 35.3 %shard_map.139 = (bf16[12,512,96]{2,1,0:T(8,128)(2,1)}, f32[96,3456]{1,0:T(8,128)}, f32[8,192,96]{2,1,0:T(8,128)}) custom-call(s32[324]{0:T(512)} %reshape.76.ids, bf16[12,512,96]{2,1,0:T(8,128)(2,1)} %copy-done.2, bf16[72,512,96]{2,1,0:T(8,128)(2,1)} %bitcast.70, f32[12,512,1]{2,1,0:T(8,128)} %copy.86.live, bf16[12,192,64]{2,1,0:T(8,128)(2,1)} %copy.96.gp, ...), custom_call_target="tpu_custom_call" | custom-call | flops 4076863488 | bytes 100000000 | tf_op jit(solution)/shard_map/pallas_call | solution.py:231
  221.4 3.4 copy.97
  225.2 1.3 collective-permute-start.5
  226.5 5.1 %collective-permute-start.4 = (bf16[1,1,8,512,96]{3,2,4,1,0:T(8,128)(2,1)S(1)}, bf16[1,1,8,512,96]{3,2,4,1,0:T(8,128)(2,1)S(1)}, u32[]{:S(2)}, u32[]{:S(2)}) collective-permute-start(bf16[1,1,8,512,96]{3,2,4,1,0:T(8,128)(2,1)S(1)} %fusion.18), channel_id=1, source_target_pairs={{0,8},{8,16},{16,24},{1,9},{9,17},{17,25},{2,10},{10,18},{18,26},{... | collective-permute-start | bytes 2359304 | tf_op jit(solution)/shard_map/ppermute | solution.py:160
  231.6 14.9 %collective-permute-done.5 = bf16[1,1,8,512,96]{3,2,4,1,0:T(8,128)(2,1)S(1)} collective-permute-done((bf16[1,1,8,512,96]{3,2,4,1,0:T(8,128)(2,1)S(1)}, bf16[1,1,8,512,96]{3,2,4,1,0:T(8,128)(2,1)S(1)}, u32[]{:S(2)}, u32[]{:S(2)}) %collective-permute-start.5) | collective-permute-done | bytes 786464 | tf_op jit(solution)/shard_map/ppermute | solution.py:161
  246.5 1.2 collective-permute-done.4
  247.7 1.7 pad_maximum_fusion.3
  249.4 1.3 collective-permute-start.7
  250.7 4.5 collective-permute-start.6
  255.1 1.5 reshape.81
  256.7 1.4 slice_bitcast_fusion
  258.0 1.1 copy-done.9
  259.1 1.1 pad.8
  260.2 4.4 fusion.3
  264.7 130.9 %all-reduce.5.cloned.1.call-done = (f32[27,96,96]{2,0,1:T(8,128)}, f32[8,192,96]{2,1,0:T(8,128)}) async-done(((f32[27,96,96]{2,0,1:T(8,128)}, f32[8,192,96]{2,1,0:T(8,128)}), (f32[27,96,96]{2,0,1:T(8,128)}, f32[8,192,96]{2,1,0:T(8,128)})) %all-reduce.5.cloned.1.call-update) | async-done | bytes 1585168 | tf_op jit(solution)/shard_map/psum | solution.py:258
  395.6 3.2 copy.101
  398.9 5.9 %pad_maximum_fusion.1 = bf16[3,3,8,512,96]{3,2,4,1,0:T(8,128)(2,1)} fusion(bf16[3,1,8,512,96]{3,2,4,1,0:T(8,128)(2,1)} %collective-permute-done.7, bf16[1,1,8,512,96]{3,2,4,1,0:T(8,128)(2,1)S(1)} %collective-permute-done.5, bf16[1,1,8,512,96]{3,2,4,1,0:T(8,128)(2,1)S(1)} %fusion.18, bf16[1,1,8,512,96]{3,2,4,1,0:T(8,128)(2,1)S(1)} %copy-done.6, ...), kind=kLoop, calls=%fused_computation.1 | loop fusion | flops 14155776 | bytes 14155776 | tf_op jit(solution)/shard_map/concatenate | solution.py:162
  404.7 11.7 %copy.98 = bf16[3,3,8,512,96]{4,3,2,1,0:T(8,128)(2,1)} copy(bf16[3,3,8,512,96]{3,2,4,1,0:T(8,128)(2,1)} %pad_maximum_fusion.1) | data formatting | bytes 14155776 | tf_op jit(solution)/shard_map/concatenate | solution.py:162
  416.4 24.4 %shard_map.140 = bf16[12,512,96]{2,1,0:T(8,128)(2,1)} custom-call(s32[324]{0:T(512)} %reshape.76.ids, bf16[12,512,96]{2,1,0:T(8,128)(2,1)} %get-tuple-element.13.own, bf16[72,512,96]{2,1,0:T(8,128)(2,1)} %bitcast.71, f32[12,512,1]{2,1,0:T(8,128)} %copy.86.live, bf16[3456,96]{1,0:T(8,128)(2,1)} %bitcast.73), custom_call_target="tpu_custom_call" | custom-call | flops 4076863488 | bytes 100000000 | tf_op jit(solution)/shard_map/pallas_call | solution.py:261
  440.8 2.6 copy.100
  443.5 0.9 copy.122
  (52 shorter events, 2.6 us)
Async XLA Ops:
  7.2 160.0 %copy-start = (bf16[8,192,512]{2,1,0:T(8,128)(2,1)S(1)}, bf16[8,192,512]{2,1,0:T(8,128)(2,1)}, u32[]{:S(2)}) copy-start(bf16[8,192,512]{2,1,0:T(8,128)(2,1)} %param.19) | copy-start | bytes 4718596
  7.2 2.6 copy-start.12
  12.0 3.1 copy-start.2
  12.0 3.1 copy-start.14
  16.9 25.5 %copy-start.3 = (bf16[1,1,8,512,96]{3,2,4,1,0:T(8,128)(2,1)}, bf16[1,1,8,512,96]{3,2,4,1,0:T(8,128)(2,1)S(1)}, u32[]{:S(2)}) copy-start(bf16[1,1,8,512,96]{3,2,4,1,0:T(8,128)(2,1)S(1)} %fusion.17) | copy-start | bytes 2359300
  16.9 31.3 %copy-start.15 = (s32[12,2]{0,1:T(2,128)S(1)}, s32[12,2]{0,1:T(2,128)}, u32[]{:S(2)}) copy-start(s32[12,2]{0,1:T(2,128)} %param.15) | copy-start | bytes 292
  17.0 31.5 %copy-start.16 = (s32[4]{0:T(128)S(1)}, s32[4]{0:T(128)}, u32[]{:S(2)}) copy-start(s32[4]{0:T(128)} %param.16) | copy-start | bytes 52
  17.0 36.2 %copy-start.13 = (s32[12,27]{1,0:T(8,128)S(1)}, s32[12,27]{1,0:T(8,128)}, u32[]{:S(2)}) copy-start(s32[12,27]{1,0:T(8,128)} %param.13) | copy-start | bytes 3892
  17.0 22.6 %collective-permute-start.1 = (bf16[1,1,8,512,96]{3,2,4,1,0:T(8,128)(2,1)S(1)}, bf16[1,1,8,512,96]{3,2,4,1,0:T(8,128)(2,1)S(1)}, u32[]{:S(2)}, u32[]{:S(2)}) collective-permute-start(bf16[1,1,8,512,96]{3,2,4,1,0:T(8,128)(2,1)S(1)} %fusion.17), channel_id=1, source_target_pairs={{8,0},{16,8},{24,16},{9,1},{17,9},{25,17},{10,2},{18,10},{26,18},{... | collective-permute-start | bytes 2359304 | tf_op jit(solution)/shard_map/ppermute | solution.py:161
  18.4 22.3 %collective-permute-start = (bf16[1,1,8,512,96]{3,2,4,1,0:T(8,128)(2,1)S(1)}, bf16[1,1,8,512,96]{3,2,4,1,0:T(8,128)(2,1)S(1)}, u32[]{:S(2)}, u32[]{:S(2)}) collective-permute-start(bf16[1,1,8,512,96]{3,2,4,1,0:T(8,128)(2,1)S(1)} %fusion.17), channel_id=1, source_target_pairs={{0,8},{8,16},{16,24},{1,9},{9,17},{17,25},{2,10},{10,18},{18,26},{... | collective-permute-start | bytes 2359304 | tf_op jit(solution)/shard_map/ppermute | solution.py:160
  40.8 1.7 copy-start.7
  42.5 18.1 %collective-permute-start.3 = (bf16[3,1,8,512,96]{3,2,4,1,0:T(8,128)(2,1)}, bf16[3,1,8,512,96]{3,2,4,1,0:T(8,128)(2,1)}, u32[]{:S(2)}, u32[]{:S(2)}) collective-permute-start(bf16[3,1,8,512,96]{3,2,4,1,0:T(8,128)(2,1)} %pad_maximum_fusion.2), channel_id=1, source_target_pairs={{1,0},{2,1},{3,2},{4,3},{5,4},{6,5},{7,6},{9,8},{10,9},{11,10},{12... | collective-permute-start | bytes 7077896 | tf_op jit(solution)/shard_map/ppermute | solution.py:161
  43.8 16.8 %collective-permute-start.2 = (bf16[3,1,8,512,96]{3,2,4,1,0:T(8,128)(2,1)}, bf16[3,1,8,512,96]{3,2,4,1,0:T(8,128)(2,1)}, u32[]{:S(2)}, u32[]{:S(2)}) collective-permute-start(bf16[3,1,8,512,96]{3,2,4,1,0:T(8,128)(2,1)} %pad_maximum_fusion.2), channel_id=1, source_target_pairs={{0,1},{1,2},{2,3},{3,4},{4,5},{5,6},{6,7},{8,9},{9,10},{10,11},{11... | collective-permute-start | bytes 7077896 | tf_op jit(solution)/shard_map/ppermute | solution.py:160
  49.3 64.6 %all-to-all-start.1 = ((bf16[8,3,8]{2,1,0:T(4,128)(2,1)}), bf16[8,3,8]{2,1,0:T(4,128)(2,1)S(1)}, u32[]{:S(2)}, u32[]{:S(2)}) async-start(bf16[8,3,8]{2,1,0:T(4,128)(2,1)} %copy.89), calls=%async_computation.1 | async-start | bytes 16384 | tf_op jit(solution)/shard_map/all_to_all | solution.py:195
  56.0 4.6 %copy-start.4 = (bf16[1,1,8,512,96]{3,2,4,1,0:T(8,128)(2,1)S(1)}, bf16[1,1,8,512,96]{3,2,4,1,0:T(8,128)(2,1)}, u32[]{:S(2)}) copy-start(bf16[1,1,8,512,96]{3,2,4,1,0:T(8,128)(2,1)} %copy-done.3) | copy-start | bytes 2359300
  58.2 2.3 copy-start.8
  113.8 53.4 %all-to-all-start = ((bf16[8,3,192,64]{2,3,1,0:T(8,128)(2,1)}), bf16[8,3,192,64]{2,3,1,0:T(8,128)(2,1)}, u32[]{:S(2)}, u32[]{:S(2)}) async-start(bf16[8,3,192,64]{2,3,1,0:T(8,128)(2,1)} %copy.88), calls=%async_computation | async-start | bytes 1572864 | tf_op jit(solution)/shard_map/all_to_all | solution.py:223
  154.5 241.1 %all-reduce.5.cloned.1.call-start = ((), (), s32[]{:S(2)}) async-start(), calls=%async_computation.3 | async-start | bytes 4718592 | tf_op jit(solution)/shard_map/psum | solution.py:258
  156.1 13.3 %copy-start.10 = (bf16[8,3,64,512]{3,0,2,1:T(8,128)(2,1)}, bf16[8,3,64,512]{3,0,2,1:T(8,128)(2,1)S(1)}, u32[]{:S(2)}) copy-start(bf16[8,3,64,512]{3,0,2,1:T(8,128)(2,1)S(1)} %convolution_convert_fusion) | copy-start | bytes 4718596
  225.2 21.3 %collective-permute-start.5 = (bf16[1,1,8,512,96]{3,2,4,1,0:T(8,128)(2,1)S(1)}, bf16[1,1,8,512,96]{3,2,4,1,0:T(8,128)(2,1)S(1)}, u32[]{:S(2)}, u32[]{:S(2)}) collective-permute-start(bf16[1,1,8,512,96]{3,2,4,1,0:T(8,128)(2,1)S(1)} %fusion.18), channel_id=1, source_target_pairs={{8,0},{16,8},{24,16},{9,1},{17,9},{25,17},{10,2},{18,10},{26,18},{... | collective-permute-start | bytes 2359304 | tf_op jit(solution)/shard_map/ppermute | solution.py:161
  226.5 21.1 %collective-permute-start.4 = (bf16[1,1,8,512,96]{3,2,4,1,0:T(8,128)(2,1)S(1)}, bf16[1,1,8,512,96]{3,2,4,1,0:T(8,128)(2,1)S(1)}, u32[]{:S(2)}, u32[]{:S(2)}) collective-permute-start(bf16[1,1,8,512,96]{3,2,4,1,0:T(8,128)(2,1)S(1)} %fusion.18), channel_id=1, source_target_pairs={{0,8},{8,16},{16,24},{1,9},{9,17},{17,25},{2,10},{10,18},{18,26},{... | collective-permute-start | bytes 2359304 | tf_op jit(solution)/shard_map/ppermute | solution.py:160
  247.7 1.7 copy-start.5
  249.4 149.5 %collective-permute-start.7 = (bf16[3,1,8,512,96]{3,2,4,1,0:T(8,128)(2,1)}, bf16[3,1,8,512,96]{3,2,4,1,0:T(8,128)(2,1)}, u32[]{:S(2)}, u32[]{:S(2)}) collective-permute-start(bf16[3,1,8,512,96]{3,2,4,1,0:T(8,128)(2,1)} %pad_maximum_fusion.3), channel_id=1, source_target_pairs={{1,0},{2,1},{3,2},{4,3},{5,4},{6,5},{7,6},{9,8},{10,9},{11,10},{12... | collective-permute-start | bytes 7077896 | tf_op jit(solution)/shard_map/ppermute | solution.py:161
  250.7 148.2 %collective-permute-start.6 = (bf16[3,1,8,512,96]{3,2,4,1,0:T(8,128)(2,1)}, bf16[3,1,8,512,96]{3,2,4,1,0:T(8,128)(2,1)}, u32[]{:S(2)}, u32[]{:S(2)}) collective-permute-start(bf16[3,1,8,512,96]{3,2,4,1,0:T(8,128)(2,1)} %pad_maximum_fusion.3), channel_id=1, source_target_pairs={{0,1},{1,2},{2,3},{3,4},{4,5},{5,6},{6,7},{8,9},{9,10},{10,11},{11... | collective-permute-start | bytes 7077896 | tf_op jit(solution)/shard_map/ppermute | solution.py:160
  258.0 1.1 copy-start.9
  264.7 134.2 %copy-start.6 = (bf16[1,1,8,512,96]{3,2,4,1,0:T(8,128)(2,1)S(1)}, bf16[1,1,8,512,96]{3,2,4,1,0:T(8,128)(2,1)}, u32[]{:S(2)}) copy-start(bf16[1,1,8,512,96]{3,2,4,1,0:T(8,128)(2,1)} %copy-done.5) | copy-start | bytes 2359300
  440.8 2.7 copy-start.11
  440.8 3.5 copy-start.1
Sparse Core Ops, SparseCore 0:
  258.2 137.4 all-reduce.4
